TPU v7x, 256 devices: a whole 4x4x8 slice. The times are simulated.
256 devices in a mesh: blk: 8 (over x_lo, y), uly: 32 (over x_hi, z, core).
Axes of the slice: x: 4 (x_hi: 2, x_lo: 2; x = x_hi * 2 + x_lo), y: 4, z: 8, core: 2. Of those that a mesh axis runs over, the one named last changes fastest.
Arguments:
- queries: bfloat16 [32768, 4096], P(('blk', 'uly')), may hold values from -8 to 8
- keys: bfloat16 [32768, 4096], P(('blk', 'uly')), may hold values from -8 to 8
- values: bfloat16 [32768, 4096], P(('blk', 'uly')), may hold values from -6 to 6
- grad_out: bfloat16 [32768, 4096], P(('blk', 'uly')), may hold values from -6 to 6
- doc_start: int32 [256], replicated, may hold values from 0 to 32640, as said below
Outputs:
- grad_queries: bfloat16 [32768, 4096], P(('blk', 'uly'))
- grad_keys: bfloat16 [32768, 4096], P(('blk', 'uly'))
- grad_values: bfloat16 [32768, 4096], P(('blk', 'uly'))
Inputs may be any that keep to these rules, and one draw needn't show every extreme that they name: `doc_start`: each entry is the first position of its block's document, so documents are runs of whole blocks; no document is longer than 8 blocks and one is exactly 8; a document crosses every boundary between groups of 4096 positions and starts at most 7 blocks before it, at one boundary exactly 7; the last block starts a document.
All inputs are finite; a program needn't handle non-finite values.
Results may differ from a plain program's by a relative error of at most 0.0051.
Values may be sent and summed in bfloat16 or wider, within the bound.
No kernel may reach another device: no remote copies, remote signals or barrier semaphores. Data moves between devices by JAX's collectives and lax.ppermute only.
A program may use at most 64 MiB of HBM per device.

v0:
```python
import math

import jax
import jax.numpy as jnp
from jax import lax
from jax.sharding import PartitionSpec as P

BLOCK = 128
MAXB = 8


def passed_along(array, axis, by):
    devices = lax.axis_size(axis)
    pairs = [(i, i + by) for i in range(devices) if 0 <= i + by < devices]
    return lax.ppermute(array, axis, pairs)


def body(queries, keys, values, grad_out, doc_start):
    q_all, k_all, v_all, d_all = (
        lax.all_to_all(queries, "uly", split_axis=1, concat_axis=0, tiled=True),
        lax.all_to_all(keys, "uly", split_axis=1, concat_axis=0, tiled=True),
        lax.all_to_all(values, "uly", split_axis=1, concat_axis=0, tiled=True),
        lax.all_to_all(grad_out, "uly", split_axis=1, concat_axis=0, tiled=True),
    )
    group_rows, width = q_all.shape
    tile = 4 * BLOCK
    fetch_rows = (MAXB - 1) * BLOCK
    lead_tiles = -(-fetch_rows // tile)
    lead_rows = lead_tiles * tile
    pad_rows = lead_rows - fetch_rows
    lead_blocks = lead_rows // BLOCK
    local_blocks = group_rows // BLOCK
    ext_rows = lead_rows + group_rows
    group = lax.axis_index("blk")
    scale = 1.0 / math.sqrt(width)
    split_at = group_rows - fetch_rows
    tail_k = k_all[split_at:]
    tail_v = v_all[split_at:]
    far_k, far_v = passed_along((tail_k, tail_v), "blk", 1)
    blank = jnp.zeros((pad_rows, width), jnp.bfloat16)
    ext_k = jnp.concatenate([blank, far_k, k_all], 0)
    ext_v = jnp.concatenate([blank, far_v, v_all], 0)
    padded_docs = jnp.concatenate([jnp.full((lead_blocks,), -1, jnp.int32), doc_start], 0)
    block_doc = lax.dynamic_slice_in_dim(
        padded_docs, group * local_blocks, lead_blocks + local_blocks, 0
    )
    block_doc = jnp.where(jnp.arange(lead_blocks + local_blocks) < pad_rows // BLOCK, -1, block_doc)
    key_doc = jnp.repeat(block_doc, BLOCK)
    first_pos = (group * local_blocks - lead_blocks) * BLOCK
    key_pos = first_pos + jnp.arange(ext_rows, dtype=jnp.int32)
    query_doc = key_doc[lead_rows:]
    query_pos = key_pos[lead_rows:]

    def query_tile(t, carry):
        dq_all, dk_ext, dv_ext, lse_all, delta_all = carry
        q_start = t * tile
        q_rows = lax.dynamic_slice_in_dim(q_all, q_start, tile, 0)
        d_rows = lax.dynamic_slice_in_dim(d_all, q_start, tile, 0)
        q_doc = lax.dynamic_slice_in_dim(query_doc, q_start, tile, 0)
        q_pos = lax.dynamic_slice_in_dim(query_pos, q_start, tile, 0)
        lower = (q_doc[0] - first_pos) // tile
        upper = t + lead_tiles + 1

        def scores(j):
            k_start = j * tile
            k_rows = lax.dynamic_slice_in_dim(ext_k, k_start, tile, 0)
            v_rows = lax.dynamic_slice_in_dim(ext_v, k_start, tile, 0)
            k_doc = lax.dynamic_slice_in_dim(key_doc, k_start, tile, 0)
            k_pos = lax.dynamic_slice_in_dim(key_pos, k_start, tile, 0)
            allowed = (q_doc[:, None] == k_doc[None, :]) & (k_pos[None, :] <= q_pos[:, None])
            score = (
                jnp.einsum("qd,kd->qk", q_rows, k_rows, preferred_element_type=jnp.float32) * scale
            )
            score = jnp.where(allowed, score, -1e30)
            dprob = jnp.einsum("qd,kd->qk", d_rows, v_rows, preferred_element_type=jnp.float32)
            return (k_rows, score, allowed, dprob)

        def first_pass(j, stats):
            top, total, cross = stats
            k_rows, score, allowed, dprob = scores(j)
            new_top = jnp.maximum(top, jnp.max(score, axis=1))
            fade = jnp.exp(top - new_top)
            weight = jnp.where(allowed, jnp.exp(score - new_top[:, None]), 0.0)
            return (
                new_top,
                total * fade + jnp.sum(weight, axis=1),
                cross * fade + jnp.sum(weight * dprob, axis=1),
            )

        start_stats = (
            jnp.full((tile,), -1e30, jnp.float32),
            jnp.zeros((tile,), jnp.float32),
            jnp.zeros((tile,), jnp.float32),
        )
        top, total, cross = lax.fori_loop(lower, upper, first_pass, start_stats)
        lse = top + jnp.log(total)
        delta = cross / total

        def tile_terms(j):
            k_rows, score, allowed, dprob = scores(j)
            prob = jnp.where(allowed, jnp.exp(score - lse[:, None]), 0.0)
            dscore = (prob * (dprob - delta[:, None]) * scale).astype(jnp.bfloat16)
            prob_low = prob.astype(jnp.bfloat16)
            return (k_rows, dscore, prob_low)

        def full_pass(j, acc):
            dq_part, dk_acc, dv_acc = acc
            k_rows, dscore, prob_low = tile_terms(j)
            dq_part = dq_part + jnp.einsum(
                "qk,kd->qd", dscore, k_rows, preferred_element_type=jnp.float32
            )
            k_start = j * tile
            dk_acc = lax.dynamic_update_slice_in_dim(
                dk_acc,
                lax.dynamic_slice_in_dim(dk_acc, k_start, tile, 0)
                + jnp.einsum("qk,qd->kd", dscore, q_rows, preferred_element_type=jnp.float32),
                k_start,
                0,
            )
            dv_acc = lax.dynamic_update_slice_in_dim(
                dv_acc,
                lax.dynamic_slice_in_dim(dv_acc, k_start, tile, 0)
                + jnp.einsum("qk,qd->kd", prob_low, d_rows, preferred_element_type=jnp.float32),
                k_start,
                0,
            )
            return (dq_part, dk_acc, dv_acc)

        start_acc = (jnp.zeros((tile, width), jnp.float32), dk_ext, dv_ext)
        dq_part, dk_ext, dv_ext = lax.fori_loop(lower, upper, full_pass, start_acc)
        dq_all = lax.dynamic_update_slice_in_dim(dq_all, dq_part.astype(jnp.bfloat16), q_start, 0)
        lse_all = lax.dynamic_update_slice_in_dim(lse_all, lse, q_start, 0)
        delta_all = lax.dynamic_update_slice_in_dim(delta_all, delta, q_start, 0)
        return (dq_all, dk_ext, dv_ext, lse_all, delta_all)

    start_carry = (
        jnp.zeros((group_rows, width), jnp.bfloat16),
        jnp.zeros((ext_rows, width), jnp.float32),
        jnp.zeros((ext_rows, width), jnp.float32),
        jnp.zeros((group_rows,), jnp.float32),
        jnp.zeros((group_rows,), jnp.float32),
    )
    dq_all, dk_ext, dv_ext, lse_all, delta_all = lax.fori_loop(
        0, group_rows // tile, query_tile, start_carry
    )
    near_k = dk_ext[pad_rows:lead_rows]
    near_v = dv_ext[pad_rows:lead_rows]
    back_k, back_v = (
        passed_along(near_k.astype(jnp.bfloat16), "blk", -1).astype(near_k.dtype),
        passed_along(near_v.astype(jnp.bfloat16), "blk", -1).astype(near_v.dtype),
    )
    own_k = dk_ext[lead_rows:]
    own_v = dv_ext[lead_rows:]
    own_k = jnp.concatenate([own_k[:split_at], own_k[split_at:] + back_k], 0).astype(jnp.bfloat16)
    own_v = jnp.concatenate([own_v[:split_at], own_v[split_at:] + back_v], 0).astype(jnp.bfloat16)
    grad_q, grad_k, grad_v = (
        lax.all_to_all(dq_all, "uly", split_axis=0, concat_axis=1, tiled=True),
        lax.all_to_all(own_k, "uly", split_axis=0, concat_axis=1, tiled=True),
        lax.all_to_all(own_v, "uly", split_axis=0, concat_axis=1, tiled=True),
    )
    return (grad_q, grad_k, grad_v)


def solution(mesh):
    return jax.shard_map(
        body,
        mesh=mesh,
        in_specs=(
            P(("blk", "uly"), None),
            P(("blk", "uly"), None),
            P(("blk", "uly"), None),
            P(("blk", "uly"), None),
            P(),
        ),
        out_specs=(P(("blk", "uly"), None), P(("blk", "uly"), None), P(("blk", "uly"), None)),
        check_vma=False,
    )
```

profile of v0, /device:TPU:58, one launch (start us, length us, event | category | flops | bytes accessed | tf_op | source)
XLA Modules:
  0.0 438.7 jit_solution(15179668549526494421)
XLA Ops:
  3.1 10.3 %all-to-all-start = ((bf16[128,32,128]{2,0,1:T(8,128)(2,1)}), bf16[128,32,128]{2,0,1:T(8,128)(2,1)S(1)}, u32[]{:S(2)}, u32[]{:S(2)}) async-start(bf16[128,32,128]{2,0,1:T(8,128)(2,1)} %copy_bitcast_fusion.3), calls=%async_computation | async-start | bytes 2097152 | tf_op jit(solution)/shard_map/all_to_all | solution.py:20
  14.7 29.2 %all-to-all-done = bf16[128,32,128]{2,0,1:T(8,128)(2,1)S(1)} async-done(((bf16[128,32,128]{2,0,1:T(8,128)(2,1)}), bf16[128,32,128]{2,0,1:T(8,128)(2,1)S(1)}, u32[]{:S(2)}, u32[]{:S(2)}) %all-to-all-start) | async-done | bytes 1048608 | tf_op jit(solution)/shard_map/all_to_all | solution.py:20
  50.1 27.7 %all-to-all-done.2 = bf16[128,32,128]{2,0,1:T(8,128)(2,1)S(1)} async-done(((bf16[128,32,128]{2,0,1:T(8,128)(2,1)}), bf16[128,32,128]{2,0,1:T(8,128)(2,1)S(1)}, u32[]{:S(2)}, u32[]{:S(2)}) %all-to-all-start.2) | async-done | bytes 1048608 | tf_op jit(solution)/shard_map/all_to_all | solution.py:21
  84.1 27.7 %all-to-all-done.3 = bf16[128,32,128]{2,0,1:T(8,128)(2,1)S(1)} async-done(((bf16[128,32,128]{2,0,1:T(8,128)(2,1)}), bf16[128,32,128]{2,0,1:T(8,128)(2,1)S(1)}, u32[]{:S(2)}, u32[]{:S(2)}) %all-to-all-start.3) | async-done | bytes 1048608 | tf_op jit(solution)/shard_map/all_to_all | solution.py:22
  119.9 7.0 %collective-permute-done = bf16[896,128]{1,0:T(8,128)(2,1)} collective-permute-done((bf16[896,128]{1,0:T(8,128)(2,1)S(1)}, bf16[896,128]{1,0:T(8,128)(2,1)}, u32[]{:S(2)}, u32[]{:S(2)}) %collective-permute-start) | collective-permute-done | bytes 229408 | tf_op jit(solution)/shard_map/ppermute | solution.py:15
  130.3 5.7 %pad_maximum_fusion.1 = (bf16[5120,128]{1,0:T(8,128)(2,1)S(1)}, bf16[5120,128]{1,0:T(8,128)(2,1)}) fusion(bf16[4096,128]{1,0:T(8,128)(2,1)} %bitcast.116, bf16[896,128]{1,0:T(8,128)(2,1)} %collective-permute-done.1, bf16[5120]{0:T(1024)(128)(2,1)S(1)} %pad.8.clone, bf16[4096,128]{1,0:T(8,128)(2,1)S(1)} %bitcast.114, bf16[896,128]{1,0:T(8,128)(2,1)} %collective-permute-done), kind=kLoop, calls=%fused_computation.48 | loop fusion | flops 7208960 | bytes 5187584 | tf_op jit(solution)/shard_map/concatenate | solution.py:42
  136.0 10.4 %all-to-all-done.1 = bf16[128,32,128]{2,0,1:T(8,128)(2,1)} async-done(((bf16[128,32,128]{2,0,1:T(8,128)(2,1)}), bf16[128,32,128]{2,0,1:T(8,128)(2,1)}, u32[]{:S(2)}, u32[]{:S(2)}) %all-to-all-start.1) | async-done | bytes 1048608 | tf_op jit(solution)/shard_map/all_to_all | solution.py:23
  150.9 183.4 %while.115 = (s32[]{:T(128)}, bf16[4096,128]{1,0:T(8,128)(2,1)}, f32[5120,128]{1,0:T(8,128)}, f32[5120,128]{1,0:T(8,128)}, s32[4096]{0:T(1024)S(1)}, /*index=5*/...) while((s32[]{:T(128)}, bf16[4096,128]{1,0:T(8,128)(2,1)}, ...), condition=%wide.region_8.9_spmd.clone.clone, body=%wide.region_0.8_spmd.clone.clone.sunk | while | flops 478158336 | bytes 12215727 | solution.py:143
  153.3 6.8 %while.116 = (s32[]{:T(128)}, f32[512]{0:T(512)S(1)}, f32[512]{0:T(512)S(1)}, f32[512]{0:T(512)S(1)}, s32[]{:T(128)}, /*index=5*/s32[512]{0:T(512)S(1)}, s32[512...) while((s32[]{:T(128)}, f32[512]{0:T(512)S(1)}, ...), condition=%wide.region_5.5_spmd, body=%wide.region_1.4_spmd.sunk | while | flops 139200000 | bytes 3739867 | solution.py:95
  160.2 21.1 %while.117 = (s32[]{:T(128)}, f32[512,128]{1,0:T(8,128)S(1)}, f32[5120,128]{1,0:T(8,128)}, f32[5120,128]{1,0:T(8,128)}, s32[]{:T(128)}, /*index=5*/s32[512]{0:T(...) while((s32[]{:T(128)}, f32[512,128]{1,0:T(8,128)S(1)}, ...), condition=%wide.region_7.7_spmd, body=%wide.region_6.6_spmd.sunk | while | flops 338886656 | bytes 7229687 | solution.py:130
  188.9 14.0 %while.117 = (s32[]{:T(128)}, f32[512,128]{1,0:T(8,128)S(1)}, f32[5120,128]{1,0:T(8,128)}, f32[5120,128]{1,0:T(8,128)}, s32[]{:T(128)}, /*index=5*/s32[512]{0:T(...) while((s32[]{:T(128)}, f32[512,128]{1,0:T(8,128)S(1)}, ...), condition=%wide.region_7.7_spmd, body=%wide.region_6.6_spmd.sunk | while | flops 338886656 | bytes 7229687 | solution.py:130
  210.6 14.0 %while.117 = (s32[]{:T(128)}, f32[512,128]{1,0:T(8,128)S(1)}, f32[5120,128]{1,0:T(8,128)}, f32[5120,128]{1,0:T(8,128)}, s32[]{:T(128)}, /*index=5*/s32[512]{0:T(...) while((s32[]{:T(128)}, f32[512,128]{1,0:T(8,128)S(1)}, ...), condition=%wide.region_7.7_spmd, body=%wide.region_6.6_spmd.sunk | while | flops 338886656 | bytes 7229687 | solution.py:130
  227.8 6.8 %while.116 = (s32[]{:T(128)}, f32[512]{0:T(512)S(1)}, f32[512]{0:T(512)S(1)}, f32[512]{0:T(512)S(1)}, s32[]{:T(128)}, /*index=5*/s32[512]{0:T(512)S(1)}, s32[512...) while((s32[]{:T(128)}, f32[512]{0:T(512)S(1)}, ...), condition=%wide.region_5.5_spmd, body=%wide.region_1.4_spmd.sunk | while | flops 139200000 | bytes 3739867 | solution.py:95
  234.6 21.1 %while.117 = (s32[]{:T(128)}, f32[512,128]{1,0:T(8,128)S(1)}, f32[5120,128]{1,0:T(8,128)}, f32[5120,128]{1,0:T(8,128)}, s32[]{:T(128)}, /*index=5*/s32[512]{0:T(...) while((s32[]{:T(128)}, f32[512,128]{1,0:T(8,128)S(1)}, ...), condition=%wide.region_7.7_spmd, body=%wide.region_6.6_spmd.sunk | while | flops 338886656 | bytes 7229687 | solution.py:130
  261.1 7.1 %while.117 = (s32[]{:T(128)}, f32[512,128]{1,0:T(8,128)S(1)}, f32[5120,128]{1,0:T(8,128)}, f32[5120,128]{1,0:T(8,128)}, s32[]{:T(128)}, /*index=5*/s32[512]{0:T(...) while((s32[]{:T(128)}, f32[512,128]{1,0:T(8,128)S(1)}, ...), condition=%wide.region_7.7_spmd, body=%wide.region_6.6_spmd.sunk | while | flops 338886656 | bytes 7229687 | solution.py:130
  275.9 14.1 %while.117 = (s32[]{:T(128)}, f32[512,128]{1,0:T(8,128)S(1)}, f32[5120,128]{1,0:T(8,128)}, f32[5120,128]{1,0:T(8,128)}, s32[]{:T(128)}, /*index=5*/s32[512]{0:T(...) while((s32[]{:T(128)}, f32[512,128]{1,0:T(8,128)S(1)}, ...), condition=%wide.region_7.7_spmd, body=%wide.region_6.6_spmd.sunk | while | flops 338886656 | bytes 7229687 | solution.py:130
  293.1 4.6 %while.116 = (s32[]{:T(128)}, f32[512]{0:T(512)S(1)}, f32[512]{0:T(512)S(1)}, f32[512]{0:T(512)S(1)}, s32[]{:T(128)}, /*index=5*/s32[512]{0:T(512)S(1)}, s32[512...) while((s32[]{:T(128)}, f32[512]{0:T(512)S(1)}, ...), condition=%wide.region_5.5_spmd, body=%wide.region_1.4_spmd.sunk | while | flops 139200000 | bytes 3739867 | solution.py:95
  297.7 14.1 %while.117 = (s32[]{:T(128)}, f32[512,128]{1,0:T(8,128)S(1)}, f32[5120,128]{1,0:T(8,128)}, f32[5120,128]{1,0:T(8,128)}, s32[]{:T(128)}, /*index=5*/s32[512]{0:T(...) while((s32[]{:T(128)}, f32[512,128]{1,0:T(8,128)S(1)}, ...), condition=%wide.region_7.7_spmd, body=%wide.region_6.6_spmd.sunk | while | flops 338886656 | bytes 7229687 | solution.py:130
  319.5 14.1 %while.117 = (s32[]{:T(128)}, f32[512,128]{1,0:T(8,128)S(1)}, f32[5120,128]{1,0:T(8,128)}, f32[5120,128]{1,0:T(8,128)}, s32[]{:T(128)}, /*index=5*/s32[512]{0:T(...) while((s32[]{:T(128)}, f32[512,128]{1,0:T(8,128)S(1)}, ...), condition=%wide.region_7.7_spmd, body=%wide.region_6.6_spmd.sunk | while | flops 338886656 | bytes 7229687 | solution.py:130
  341.3 5.1 %collective-permute-done.3 = bf16[896,128]{1,0:T(8,128)(2,1)S(1)} collective-permute-done((bf16[896,128]{1,0:T(8,128)(2,1)S(1)}, bf16[896,128]{1,0:T(8,128)(2,1)S(1)}, u32[]{:S(2)}, u32[]{:S(2)}) %collective-permute-start.3) | collective-permute-done | bytes 229408 | tf_op jit(solution)/shard_map/ppermute | solution.py:15
  348.5 19.8 %all-to-all-done.4 = bf16[32,128,128]{2,1,0:T(8,128)(2,1)S(1)} async-done(((bf16[32,128,128]{2,1,0:T(8,128)(2,1)}), bf16[32,128,128]{2,1,0:T(8,128)(2,1)S(1)}, u32[]{:S(2)}, u32[]{:S(2)}) %all-to-all-start.4) | async-done | bytes 1048608 | tf_op jit(solution)/shard_map/all_to_all | solution.py:157
  376.0 4.8 %collective-permute-done.2 = bf16[896,128]{1,0:T(8,128)(2,1)S(1)} collective-permute-done((bf16[896,128]{1,0:T(8,128)(2,1)S(1)}, bf16[896,128]{1,0:T(8,128)(2,1)S(1)}, u32[]{:S(2)}, u32[]{:S(2)}) %collective-permute-start.2) | collective-permute-done | bytes 229408 | tf_op jit(solution)/shard_map/ppermute | solution.py:15
  382.9 19.9 %all-to-all-done.6 = bf16[32,128,128]{2,1,0:T(8,128)(2,1)} async-done(((bf16[32,128,128]{2,1,0:T(8,128)(2,1)}), bf16[32,128,128]{2,1,0:T(8,128)(2,1)}, u32[]{:S(2)}, u32[]{:S(2)}) %all-to-all-start.6) | async-done | bytes 1048608 | tf_op jit(solution)/shard_map/all_to_all | solution.py:159
  413.0 23.7 %all-to-all-done.5 = bf16[32,128,128]{2,1,0:T(8,128)(2,1)S(1)} async-done(((bf16[32,128,128]{2,1,0:T(8,128)(2,1)}), bf16[32,128,128]{2,1,0:T(8,128)(2,1)S(1)}, u32[]{:S(2)}, u32[]{:S(2)}) %all-to-all-start.5) | async-done | bytes 1048608 | tf_op jit(solution)/shard_map/all_to_all | solution.py:158
  (408 shorter events, 259.8 us)
Async XLA Ops:
  0.6 1.2 copy-start
  0.6 12.8 %copy-start.3 = (bf16[128,4096]{1,0:T(8,128)(2,1)S(1)}, bf16[128,4096]{1,0:T(8,128)(2,1)}, u32[]{:S(2)}) copy-start(bf16[128,4096]{1,0:T(8,128)(2,1)} %param.12) | copy-start | bytes 3145732
  3.1 40.8 %all-to-all-start = ((bf16[128,32,128]{2,0,1:T(8,128)(2,1)}), bf16[128,32,128]{2,0,1:T(8,128)(2,1)S(1)}, u32[]{:S(2)}, u32[]{:S(2)}) async-start(bf16[128,32,128]{2,0,1:T(8,128)(2,1)} %copy_bitcast_fusion.3), calls=%async_computation | async-start | bytes 2097152 | tf_op jit(solution)/shard_map/all_to_all | solution.py:20
  43.9 34.0 %copy-start.2 = (bf16[128,32,128]{2,0,1:T(8,128)(2,1)}, bf16[128,32,128]{2,0,1:T(8,128)(2,1)S(1)}, u32[]{:S(2)}) copy-start(bf16[128,32,128]{2,0,1:T(8,128)(2,1)S(1)} %all-to-all-done) | copy-start | bytes 3145732
  43.9 34.0 %all-to-all-start.2 = ((bf16[128,32,128]{2,0,1:T(8,128)(2,1)}), bf16[128,32,128]{2,0,1:T(8,128)(2,1)S(1)}, u32[]{:S(2)}, u32[]{:S(2)}) async-start(bf16[128,32,128]{2,0,1:T(8,128)(2,1)} %copy_bitcast_fusion.1), calls=%async_computation.2 | async-start | bytes 2097152 | tf_op jit(solution)/shard_map/all_to_all | solution.py:21
  77.9 34.0 %all-to-all-start.3 = ((bf16[128,32,128]{2,0,1:T(8,128)(2,1)}), bf16[128,32,128]{2,0,1:T(8,128)(2,1)S(1)}, u32[]{:S(2)}, u32[]{:S(2)}) async-start(bf16[128,32,128]{2,0,1:T(8,128)(2,1)} %copy_bitcast_fusion), calls=%async_computation.3 | async-start | bytes 2097152 | tf_op jit(solution)/shard_map/all_to_all | solution.py:22
  81.6 38.1 %copy-start.4 = (s32[256]{0:T(256)S(1)}, s32[256]{0:T(256)}, u32[]{:S(2)}) copy-start(s32[256]{0:T(256)} %param.15) | copy-start | bytes 3076
  111.8 18.5 %copy-start.1 = (bf16[128,32,128]{2,0,1:T(8,128)(2,1)}, bf16[128,32,128]{2,0,1:T(8,128)(2,1)S(1)}, u32[]{:S(2)}) copy-start(bf16[128,32,128]{2,0,1:T(8,128)(2,1)S(1)} %all-to-all-done.3) | copy-start | bytes 3145732
  111.8 34.5 %all-to-all-start.1 = ((bf16[128,32,128]{2,0,1:T(8,128)(2,1)}), bf16[128,32,128]{2,0,1:T(8,128)(2,1)}, u32[]{:S(2)}, u32[]{:S(2)}) async-start(bf16[128,32,128]{2,0,1:T(8,128)(2,1)} %copy_bitcast_fusion.2), calls=%async_computation.1 | async-start | bytes 2097152 | tf_op jit(solution)/shard_map/all_to_all | solution.py:23
  116.4 10.5 %collective-permute-start = (bf16[896,128]{1,0:T(8,128)(2,1)S(1)}, bf16[896,128]{1,0:T(8,128)(2,1)}, u32[]{:S(2)}, u32[]{:S(2)}) collective-permute-start(bf16[896,128]{1,0:T(8,128)(2,1)S(1)} %bitcast.122), channel_id=1, source_target_pairs={{0,32},{32,64},{64,96},{96,128},{128,160},{160,192},{192,224},{1,3... | collective-permute-start | bytes 688136 | tf_op jit(solution)/shard_map/ppermute | solution.py:15
  118.4 12.0 %collective-permute-start.1 = (bf16[896,128]{1,0:T(8,128)(2,1)}, bf16[896,128]{1,0:T(8,128)(2,1)}, u32[]{:S(2)}, u32[]{:S(2)}) collective-permute-start(bf16[896,128]{1,0:T(8,128)(2,1)} %bitcast.13), channel_id=1, source_target_pairs={{0,32},{32,64},{64,96},{96,128},{128,160},{160,192},{192,224},{1,3... | collective-permute-start | bytes 688136 | tf_op jit(solution)/shard_map/ppermute | solution.py:15
  334.3 34.0 %all-to-all-start.4 = ((bf16[32,128,128]{2,1,0:T(8,128)(2,1)}), bf16[32,128,128]{2,1,0:T(8,128)(2,1)S(1)}, u32[]{:S(2)}, u32[]{:S(2)}) async-start(bf16[32,128,128]{2,1,0:T(8,128)(2,1)} %bitcast.117), calls=%async_computation.4 | async-start | bytes 2097152 | tf_op jit(solution)/shard_map/all_to_all | solution.py:157
  339.9 6.5 %collective-permute-start.3 = (bf16[896,128]{1,0:T(8,128)(2,1)S(1)}, bf16[896,128]{1,0:T(8,128)(2,1)S(1)}, u32[]{:S(2)}, u32[]{:S(2)}) collective-permute-start(bf16[896,128]{1,0:T(8,128)(2,1)S(1)} %slice.80), channel_id=1, source_target_pairs={{32,0},{64,32},{96,64},{128,96},{160,128},{192,160},{224,192},{33,... | collective-permute-start | bytes 688136 | tf_op jit(solution)/shard_map/ppermute | solution.py:15
  368.3 34.5 %all-to-all-start.6 = ((bf16[32,128,128]{2,1,0:T(8,128)(2,1)}), bf16[32,128,128]{2,1,0:T(8,128)(2,1)}, u32[]{:S(2)}, u32[]{:S(2)}) async-start(bf16[32,128,128]{2,1,0:T(8,128)(2,1)} %bitcast.21), calls=%async_computation.6 | async-start | bytes 2097152 | tf_op jit(solution)/shard_map/all_to_all | solution.py:159
  374.6 6.1 %collective-permute-start.2 = (bf16[896,128]{1,0:T(8,128)(2,1)S(1)}, bf16[896,128]{1,0:T(8,128)(2,1)S(1)}, u32[]{:S(2)}, u32[]{:S(2)}) collective-permute-start(bf16[896,128]{1,0:T(8,128)(2,1)S(1)} %slice.78), channel_id=1, source_target_pairs={{32,0},{64,32},{96,64},{128,96},{160,128},{192,160},{224,192},{33,... | collective-permute-start | bytes 688136 | tf_op jit(solution)/shard_map/ppermute | solution.py:15
  402.8 34.0 %all-to-all-start.5 = ((bf16[32,128,128]{2,1,0:T(8,128)(2,1)}), bf16[32,128,128]{2,1,0:T(8,128)(2,1)S(1)}, u32[]{:S(2)}, u32[]{:S(2)}) async-start(bf16[32,128,128]{2,1,0:T(8,128)(2,1)} %bitcast.18), calls=%async_computation.5 | async-start | bytes 2097152 | tf_op jit(solution)/shard_map/all_to_all | solution.py:158
where the time goes:
time: 442 us; the launch traced here: 439 us
  waiting for transfers between devices  179 us (40%)
  matrix products  146 us (33%)
  local copies, waits for them, and re-layouts  42 us (10%)
  starting transfers between devices  39.3 us (9%)
  other arithmetic  24.9 us (6%)
  loops' own time  7.28 us (2%)
    dot_general x34, matrix products, scores(): jnp.einsum('qd,kd->qk', q_rows, k_rows, preferred_element_type=jnp.float32)  45 us
    dot_general x17, matrix products, full_pass(): jnp.einsum('qk,qd->kd', prob_low, d_rows, preferred_element_type=jnp.floa...  33.4 us
    dot_general x17, matrix products, full_pass(): jnp.einsum('qk,qd->kd', dscore, q_rows, preferred_element_type=jnp.float32)  33.1 us
    all_to_all x1, waiting for transfers between devices, body(): lax.all_to_all(queries, 'uly', split_axis=1, concat_axis=0, tiled=True)  29.2 us
    all_to_all x1, waiting for transfers between devices, body(): lax.all_to_all(keys, 'uly', split_axis=1, concat_axis=0, tiled=True)  27.7 us
    all_to_all x1, waiting for transfers between devices, body(): lax.all_to_all(values, 'uly', split_axis=1, concat_axis=0, tiled=True)  27.7 us
    all_to_all x1, waiting for transfers between devices, body(): lax.all_to_all(own_k, 'uly', split_axis=0, concat_axis=1, tiled=True)  23.7 us
    dot_general x17, matrix products, full_pass(): jnp.einsum('qk,kd->qd', dscore, k_rows, preferred_element_type=jnp.float32)  21.7 us
  transfers between devices with their start and end apart: 11, of which 11 were waited for; matrix products, arithmetic and copies ran while one was open for 6% of the time, Pallas kernels for 0%

commit v1 on v0

v1 whole, which is shorter than its diff:
```python
import functools
import math

import jax
import jax.numpy as jnp
from jax import lax
from jax.experimental import pallas as pl
from jax.experimental.pallas import tpu as pltpu
from jax.sharding import PartitionSpec as P

BLOCK = 128
MAXB = 8
REACH = MAXB - 1
EDGE = 8
MASKED = -1e30
LOG2E = 1.4426950408889634
F32 = jnp.float32
BF16 = jnp.bfloat16
QUERY, DOUT, KEY, VALUE = 0, 1, 2, 3
GKEY, GVALUE, GQUERY = 0, 1, 2


def across(a, b):
    return lax.dot_general(a, b, (((1,), (1,)), ((), ())), preferred_element_type=F32)


def down(a, b):
    return lax.dot_general(a, b, (((0,), (0,)), ((), ())), preferred_element_type=F32)


def plain(a, b):
    return jnp.dot(a, b, preferred_element_type=F32)


def query_pair(n, lead, second, q, d, k, v):
    width = q.shape[-1]
    scale = 1.0 / math.sqrt(width)
    rows = n * BLOCK
    s = across(k, q)
    r = lax.broadcasted_iota(jnp.int32, (rows, 2 * BLOCK), 0)
    c = lax.broadcasted_iota(jnp.int32, (1, 2 * BLOCK), 1)
    low = jnp.where(c < BLOCK, 0, second * BLOCK)
    high = c + (n - 2) * BLOCK
    s = jnp.where((r >= low) & (r <= high), s, MASKED)
    top = jnp.max(s, axis=0, keepdims=True)
    w = jnp.exp2((s - top) * (scale * LOG2E))
    total = jnp.sum(w, axis=0, keepdims=True)
    dp = across(v, d)
    cross = jnp.sum(w * dp, axis=0, keepdims=True)
    inv = 1.0 / total
    delta = cross * inv
    prob = w * inv
    ds = (prob * (dp - delta) * scale).astype(BF16)
    gv = plain(prob.astype(BF16), d)
    gk = plain(ds, q)
    gq = down(ds, k)
    lse = top * (scale * LOG2E) + jnp.log2(total)
    return gq, gk, gv, lse, delta


def inner_kernel(st_ref, x_ref, out_ref, head_ref, tail_ref, gk_ref, gv_ref):
    blocks = x_ref.shape[0]
    width = x_ref.shape[-1]
    gk_ref[...] = jnp.zeros_like(gk_ref)
    gv_ref[...] = jnp.zeros_like(gv_ref)

    def tile(t, _):
        first = st_ref[2 * t]
        n_dyn = 2 * t + 2 - first
        second = st_ref[2 * t + 1] - first
        for n in range(2, MAXB + 2):

            @pl.when((first >= 0) & (n_dyn == n))
            def _():
                window = pl.ds(first, n)
                pair = pl.ds(2 * t, 2)
                gq, gk, gv, _, _ = query_pair(
                    n,
                    0,
                    second,
                    x_ref[pair, QUERY].reshape(2 * BLOCK, width),
                    x_ref[pair, DOUT].reshape(2 * BLOCK, width),
                    x_ref[window, KEY].reshape(n * BLOCK, width),
                    x_ref[window, VALUE].reshape(n * BLOCK, width),
                )
                gk_ref[window] += gk.reshape(n, BLOCK, width)
                gv_ref[window] += gv.reshape(n, BLOCK, width)
                out_ref[pair, GQUERY] = gq.astype(BF16).reshape(2, BLOCK, width)

        return 0

    lax.fori_loop(0, blocks // 2, tile, 0)

    def store(i, _):
        out_ref[i, GKEY] = gk_ref[i].astype(BF16)
        out_ref[i, GVALUE] = gv_ref[i].astype(BF16)
        return 0

    lax.fori_loop(0, blocks, store, 0)
    head_ref[:, GKEY] = gk_ref[:EDGE]
    head_ref[:, GVALUE] = gv_ref[:EDGE]
    tail_ref[:, GKEY] = gk_ref[blocks - EDGE :]
    tail_ref[:, GVALUE] = gv_ref[blocks - EDGE :]


def head_kernel(
    st_ref, x_ref, far_ref, head_ref, out_in_ref, out_ref, stat_ref, k_ref, v_ref, gk_ref, gv_ref
):
    width = x_ref.shape[-1]
    k_ref[:REACH] = far_ref[:, 0]
    v_ref[:REACH] = far_ref[:, 1]
    k_ref[REACH:] = x_ref[:, KEY]
    v_ref[REACH:] = x_ref[:, VALUE]
    gk_ref[REACH:] = head_ref[:, GKEY]
    gv_ref[REACH:] = head_ref[:, GVALUE]
    out_ref[:, GQUERY] = out_in_ref[:, GQUERY]
    stat_ref[...] = jnp.full(stat_ref.shape, -MASKED, F32)

    def tile(t, _):
        first = st_ref[2 * t]
        n_dyn = 2 * t + 2 - first
        second = st_ref[2 * t + 1] - first
        for n in range(3, MAXB + 2):

            @pl.when((first < 0) & (n_dyn == n))
            def _():
                window = pl.ds(first + REACH, n)
                pair = pl.ds(2 * t, 2)
                gq, gk, gv, lse, delta = query_pair(
                    n,
                    0,
                    second,
                    x_ref[pair, QUERY].reshape(2 * BLOCK, width),
                    x_ref[pair, DOUT].reshape(2 * BLOCK, width),
                    k_ref[window].reshape(n * BLOCK, width),
                    v_ref[window].reshape(n * BLOCK, width),
                )
                gk_ref[window] += gk.reshape(n, BLOCK, width)
                gv_ref[window] += gv.reshape(n, BLOCK, width)
                out_ref[pair, GQUERY] = gq.astype(BF16).reshape(2, BLOCK, width)
                c = lax.broadcasted_iota(jnp.int32, lse.shape, 1)
                lse = jnp.where((c < BLOCK) | (second == 0), lse, -MASKED)
                stat_ref[t, 0:1, :] = lse
                stat_ref[t, 1:2, :] = delta

        return 0

    lax.fori_loop(0, EDGE // 2, tile, 0)
    out_ref[:, GKEY] = gk_ref[REACH:].astype(BF16)
    out_ref[:, GVALUE] = gv_ref[REACH:].astype(BF16)


def tail_kernel(st_ref, x_ref, near_ref, stat_ref, tail_ref, out_in_ref, out_ref, gk_ref, gv_ref):
    del out_in_ref
    width = x_ref.shape[-1]
    scale = 1.0 / math.sqrt(width)
    gk_ref[...] = tail_ref[:, GKEY]
    gv_ref[...] = tail_ref[:, GVALUE]
    rows = REACH * BLOCK
    q = near_ref[:, 0].reshape(rows, width)
    d = near_ref[:, 1].reshape(rows, width)
    lse = jnp.concatenate([stat_ref[t, 0:1, :] for t in range(EDGE // 2)], 1)[:, :rows]
    delta = jnp.concatenate([stat_ref[t, 1:2, :] for t in range(EDGE // 2)], 1)[:, :rows]
    live = lse < -MASKED
    delta = jnp.where(live, delta, 0.0)

    def key_block(j, _):
        s = across(x_ref[j, KEY], q)
        dp = across(x_ref[j, VALUE], d)
        prob = jnp.exp2(s * (scale * LOG2E) - lse)
        ds = (prob * (dp - delta) * scale).astype(BF16)
        gv_ref[j] += plain(prob.astype(BF16), d)
        gk_ref[j] += plain(ds, q)
        return 0

    lax.fori_loop(st_ref[st_ref.shape[0] - 1], EDGE, key_block, 0)
    out_ref[:, GKEY] = gk_ref[...].astype(BF16)
    out_ref[:, GVALUE] = gv_ref[...].astype(BF16)


def whole():
    return pl.BlockSpec(memory_space=pltpu.VMEM)


def passed_along(array, axis, by):
    devices = lax.axis_size(axis)
    pairs = [(i, i + by) for i in range(devices) if 0 <= i + by < devices]
    return lax.ppermute(array, axis, pairs)


def body(queries, keys, values, grad_out, doc_start):
    ulys = lax.axis_size("uly")
    rows, columns = queries.shape
    width = columns // ulys
    blocks = ulys * rows // BLOCK
    group = lax.axis_index("blk")
    last = lax.axis_size("blk") - 1

    packed = jnp.stack(
        [a.reshape(rows, ulys, width) for a in (queries, grad_out, keys, values)], 0
    ).transpose(2, 0, 1, 3)
    x = lax.all_to_all(packed, "uly", split_axis=0, concat_axis=0, tiled=True)

    own = lax.dynamic_slice_in_dim(doc_start, group * blocks, blocks, 0) // BLOCK - group * blocks
    after = lax.dynamic_slice_in_dim(doc_start, jnp.minimum(group + 1, last) * blocks, 1, 0) // BLOCK
    after = jnp.where(group == last, EDGE, after - group * blocks - (blocks - EDGE))
    starts = jnp.concatenate([own, after]).astype(jnp.int32)

    far = passed_along(x[blocks - REACH :, KEY : VALUE + 1], "blk", 1)
    near = passed_along(x[:REACH, QUERY : DOUT + 1], "blk", -1)

    smem = pl.BlockSpec(memory_space=pltpu.SMEM)
    params = pltpu.CompilerParams(vmem_limit_bytes=48 * 1024 * 1024)
    tile_shape = (BLOCK, width)
    out_type = jax.ShapeDtypeStruct((blocks, 3) + tile_shape, BF16)
    edge_type = jax.ShapeDtypeStruct((EDGE, 2) + tile_shape, F32)
    out, head_acc, tail_acc = pl.pallas_call(
        inner_kernel,
        out_shape=(out_type, edge_type, edge_type),
        in_specs=[smem, whole()],
        out_specs=(whole(), whole(), whole()),
        scratch_shapes=[pltpu.VMEM((blocks,) + tile_shape, F32)] * 2,
        compiler_params=params,
        cost_estimate=pl.CostEstimate(
            flops=10 * 120 * BLOCK**3 * 4, bytes_accessed=9 << 20, transcendentals=120 << 14
        ),
        name="inner",
    )(starts, x)

    def edge_in(kinds, at):
        return pl.BlockSpec((EDGE, kinds) + tile_shape, lambda i: (at, 0, 0, 0))

    def full(shape):
        return pl.BlockSpec(shape, lambda i: (0,) * len(shape))

    stat_shape = (EDGE // 2, 8, 2 * BLOCK)
    out, stats = pl.pallas_call(
        head_kernel,
        grid=(1,),
        out_shape=(out_type, jax.ShapeDtypeStruct(stat_shape, F32)),
        in_specs=[
            smem,
            edge_in(4, 0),
            full((REACH, 2) + tile_shape),
            full((EDGE, 2) + tile_shape),
            edge_in(3, 0),
        ],
        out_specs=(edge_in(3, 0), full(stat_shape)),
        scratch_shapes=[pltpu.VMEM((REACH + EDGE,) + tile_shape, BF16)] * 2
        + [pltpu.VMEM((REACH + EDGE,) + tile_shape, F32)] * 2,
        input_output_aliases={4: 0},
        compiler_params=params,
        name="head",
    )(starts, x, far, head_acc, out)
    stats = passed_along(stats, "blk", -1)
    at_end = blocks // EDGE - 1
    out = pl.pallas_call(
        tail_kernel,
        grid=(1,),
        out_shape=out_type,
        in_specs=[
            smem,
            edge_in(4, at_end),
            full((REACH, 2) + tile_shape),
            full(stat_shape),
            full((EDGE, 2) + tile_shape),
            pl.BlockSpec(memory_space=pl.ANY),
        ],
        out_specs=edge_in(2, at_end),
        scratch_shapes=[pltpu.VMEM((EDGE,) + tile_shape, F32)] * 2,
        input_output_aliases={5: 0},
        compiler_params=params,
        name="tail",
    )(starts, x, near, stats, tail_acc, out)

    back = lax.all_to_all(out, "uly", split_axis=0, concat_axis=0, tiled=True)
    back = back.transpose(1, 2, 0, 3).reshape(3, rows, columns)
    return back[GQUERY], back[GKEY], back[GVALUE]


def solution(mesh):
    part = P(("blk", "uly"), None)
    return jax.shard_map(
        body,
        mesh=mesh,
        in_specs=(part, part, part, part, P()),
        out_specs=(part, part, part),
        check_vma=False,
    )
```

time: 442 us -> 249 us (0.56)
  the two profiles are of different devices: /device:TPU:58 before, /device:TPU:23 now
where the time goes in v1:
time: 249 us; the launch traced here: 246 us
  waiting for transfers between devices  93.4 us (38%)
  blocking collectives  82.6 us (33%)
  Pallas kernels  22.3 us (9%)
  local copies, waits for them, and re-layouts  20.4 us (8%)
  starting transfers between devices  20.1 us (8%)
  other arithmetic  3.6 us (1%)
  between operations  3.42 us (1%)
    all_to_all x1, waiting for transfers between devices, body(): x = lax.all_to_all(packed, 'uly', split_axis=0, concat_axis=0, tiled=True)  90.1 us
    all_to_all x1, blocking collectives, body(): back = lax.all_to_all(out, 'uly', split_axis=0, concat_axis=0, tiled=True)  82.6 us
    pallas_call x1, Pallas kernels, body(): pl.pallas_call(inner_kernel, out_shape=(out_type, edge_type, edge_type),...  14.6 us
    all_to_all x1, starting transfers between devices, body(): x = lax.all_to_all(packed, 'uly', split_axis=0, concat_axis=0, tiled=True)  12.1 us
    unnamed x9, local copies, waits for them, and re-layouts  10.4 us
    ppermute x3, starting transfers between devices, passed_along(): return lax.ppermute(array, axis, pairs)  8.05 us
  transfers between devices with their start and end apart: 4, of which 2 were waited for; matrix products, arithmetic and copies ran while one was open for 0% of the time, Pallas kernels for 7%

profile of v1, /device:TPU:23, one launch (start us, length us, event | category | flops | bytes accessed | tf_op | source)
XLA Modules:
  0.0 245.7 jit_solution(2339664295695575069)
XLA Ops:
  0.6 1.6 copy.10
  2.3 0.7 copy.14
  2.9 1.6 copy.12
  5.2 1.6 copy.13
  6.8 1.3 copy.17
  8.2 1.6 copy.11
  9.8 1.3 copy.15
  11.1 3.4 %maximum_bitcast_fusion = bf16[32,4,128,128]{3,2,1,0:T(8,128)(2,1)} fusion(bf16[1,128,32,128]{3,1,0,2:T(8,128)(2,1)} %copy.17, bf16[1,128,32,128]{3,1,0,2:T(8,128)(2,1)S(1)} %copy.16, bf16[1,128,32,128]{3,1,0,2:T(8,128)(2,1)} %copy.15, bf16[1,128,32,128]{3,1,0,2:T(8,128)(2,1)S(1)} %copy.14), kind=kLoop, calls=%fused_computation | loop fusion | flops 6291456 | bytes 8388608 | tf_op jit(solution)/shard_map/transpose | solution.py:201
  14.5 12.1 %all-to-all-start = ((bf16[32,4,128,128]{3,2,1,0:T(8,128)(2,1)}), bf16[32,4,128,128]{3,2,1,0:T(8,128)(2,1)}, u32[]{:S(2)}, u32[]{:S(2)}) async-start(bf16[32,4,128,128]{3,2,1,0:T(8,128)(2,1)} %maximum_bitcast_fusion), calls=%async_computation | async-start | bytes 8388608 | tf_op jit(solution)/shard_map/all_to_all | solution.py:202
  30.0 90.1 %all-to-all-done.x_ref = bf16[32,4,128,128]{3,2,1,0:T(8,128)(2,1)} async-done(((bf16[32,4,128,128]{3,2,1,0:T(8,128)(2,1)}), bf16[32,4,128,128]{3,2,1,0:T(8,128)(2,1)}, u32[]{:S(2)}, u32[]{:S(2)}) %all-to-all-start) | async-done | bytes 4194336 | tf_op jit(solution)/shard_map/all_to_all | solution.py:202
  120.1 1.2 fusion.1
  121.4 2.9 %collective-permute-start.1 = (bf16[7,2,128,128]{3,2,1,0:T(8,128)(2,1)S(1)}, bf16[7,2,128,128]{3,2,1,0:T(8,128)(2,1)S(1)}, u32[]{:S(2)}, u32[]{:S(2)}) collective-permute-start(bf16[7,2,128,128]{3,2,1,0:T(8,128)(2,1)S(1)} %get-tuple-element.16), channel_id=1, source_target_pairs={{0,32},{32,64},{64,96},{96,128},{128,160},{160,192},{192,224},{1,3... | collective-permute-start | bytes 1376264 | tf_op jit(solution)/shard_map/ppermute | solution.py:188
  124.3 2.4 collective-permute-start
  126.7 14.6 %inner.1 = (bf16[32,3,128,128]{3,2,1,0:T(8,128)(2,1)S(1)}, f32[8,2,128,128]{3,2,1,0:T(8,128)S(1)}, f32[8,2,128,128]{3,2,1,0:T(8,128)S(1)}) custom-call(s32[33]{0:T(128)S(1)} %pad_add_fusion.st_ref, bf16[32,4,128,128]{3,2,1,0:T(8,128)(2,1)} %all-to-all-done.x_ref), custom_call_target="tpu_custom_call" | custom-call | flops 10066329600 | bytes 9437184 | tf_op jit(solution)/shard_map/inner/pallas_call | solution.py:217
  141.3 3.2 %head.1 = (bf16[32,3,128,128]{3,2,1,0:T(8,128)(2,1)S(1)}, f32[4,8,256]{2,1,0:T(8,128)S(1)}) custom-call(s32[33]{0:T(128)S(1)} %pad_add_fusion.st_ref, bf16[32,4,128,128]{3,2,1,0:T(8,128)(2,1)} %all-to-all-done.x_ref, bf16[7,2,128,128]{3,2,1,0:T(8,128)(2,1)S(1)} %collective-permute-done.1.far_ref, ...), custom_call_target="tpu_custom_call", output_to_operand_aliasing={{0}: (4, {})} | custom-call | tf_op jit(solution)/shard_map/head/pallas_call | solution.py:237
  144.6 2.8 %collective-permute-start.2 = (f32[4,8,256]{2,1,0:T(8,128)S(1)}, f32[4,8,256]{2,1,0:T(8,128)S(1)}, u32[]{:S(2)}, u32[]{:S(2)}) collective-permute-start(f32[4,8,256]{2,1,0:T(8,128)S(1)} %get-tuple-element.10), channel_id=1, source_target_pairs={{32,0},{64,32},{96,64},{128,96},{160,128},{192,160},{224,192},{33,... | collective-permute-start | bytes 98312 | tf_op jit(solution)/shard_map/ppermute | solution.py:188
  147.3 3.3 %collective-permute-done.2.stat_ref = f32[4,8,256]{2,1,0:T(8,128)S(1)} collective-permute-done((f32[4,8,256]{2,1,0:T(8,128)S(1)}, f32[4,8,256]{2,1,0:T(8,128)S(1)}, u32[]{:S(2)}, u32[]{:S(2)}) %collective-permute-start.2) | collective-permute-done | bytes 32800 | tf_op jit(solution)/shard_map/ppermute | solution.py:188
  150.6 4.4 %tail.1 = bf16[32,3,128,128]{3,2,1,0:T(8,128)(2,1)S(1)} custom-call(s32[33]{0:T(128)S(1)} %pad_add_fusion.st_ref, bf16[32,4,128,128]{3,2,1,0:T(8,128)(2,1)} %all-to-all-done.x_ref, bf16[7,2,128,128]{3,2,1,0:T(8,128)(2,1)S(1)} %collective-permute-done.near_ref, f32[4,8,256]{2,1,0:T(8,128)S(1)} %collective-permute-done.2.stat_ref, ...), custom_call_target="tpu_custom_call", output_to_operand_aliasing={{}: (5, {})} | custom-call | tf_op jit(solution)/shard_map/tail/pallas_call | solution.py:257
  155.0 82.6 %all_to_all.10 = bf16[32,3,128,128]{3,2,1,0:T(8,128)(2,1)S(1)} all-to-all(bf16[32,3,128,128]{3,2,1,0:T(8,128)(2,1)S(1)} %tail.1), channel_id=1, replica_groups=mesh['blk'=8,'uly'=32] {'uly'}, dimensions={0} | all-to-all | bytes 6291456 | tf_op jit(solution)/shard_map/all_to_all | solution.py:276
  237.6 1.3 fusion.2
  238.9 1.6 copy.20
  240.5 1.3 copy.23
  242.5 1.3 copy.22
  244.4 1.3 copy.21
  (10 shorter events, 2.7 us)
Async XLA Ops:
  14.5 12.1 %copy-start = (s32[256]{0:T(256)S(1)}, s32[256]{0:T(256)}, u32[]{:S(2)}) copy-start(s32[256]{0:T(256)} %param.9) | copy-start | bytes 3076
  14.5 105.6 %all-to-all-start = ((bf16[32,4,128,128]{3,2,1,0:T(8,128)(2,1)}), bf16[32,4,128,128]{3,2,1,0:T(8,128)(2,1)}, u32[]{:S(2)}, u32[]{:S(2)}) async-start(bf16[32,4,128,128]{3,2,1,0:T(8,128)(2,1)} %maximum_bitcast_fusion), calls=%async_computation | async-start | bytes 8388608 | tf_op jit(solution)/shard_map/all_to_all | solution.py:202
  121.4 19.9 %collective-permute-start.1 = (bf16[7,2,128,128]{3,2,1,0:T(8,128)(2,1)S(1)}, bf16[7,2,128,128]{3,2,1,0:T(8,128)(2,1)S(1)}, u32[]{:S(2)}, u32[]{:S(2)}) collective-permute-start(bf16[7,2,128,128]{3,2,1,0:T(8,128)(2,1)S(1)} %get-tuple-element.16), channel_id=1, source_target_pairs={{0,32},{32,64},{64,96},{96,128},{128,160},{160,192},{192,224},{1,3... | collective-permute-start | bytes 1376264 | tf_op jit(solution)/shard_map/ppermute | solution.py:188
  124.3 23.0 %collective-permute-start = (bf16[7,2,128,128]{3,2,1,0:T(8,128)(2,1)S(1)}, bf16[7,2,128,128]{3,2,1,0:T(8,128)(2,1)S(1)}, u32[]{:S(2)}, u32[]{:S(2)}) collective-permute-start(bf16[7,2,128,128]{3,2,1,0:T(8,128)(2,1)S(1)} %get-tuple-element.17), channel_id=1, source_target_pairs={{32,0},{64,32},{96,64},{128,96},{160,128},{192,160},{224,192},{33,... | collective-permute-start | bytes 1376264 | tf_op jit(solution)/shard_map/ppermute | solution.py:188
  144.6 6.0 %collective-permute-start.2 = (f32[4,8,256]{2,1,0:T(8,128)S(1)}, f32[4,8,256]{2,1,0:T(8,128)S(1)}, u32[]{:S(2)}, u32[]{:S(2)}) collective-permute-start(f32[4,8,256]{2,1,0:T(8,128)S(1)} %get-tuple-element.10), channel_id=1, source_target_pairs={{32,0},{64,32},{96,64},{128,96},{160,128},{192,160},{224,192},{33,... | collective-permute-start | bytes 98312 | tf_op jit(solution)/shard_map/ppermute | solution.py:188

commit v2 on v1

--- a/solution.py
+++ b/solution.py
@@ -178,52 +178,86 @@
     out_ref[:, GVALUE] = gv_ref[...].astype(BF16)
 
 
+def pack_kernel(*refs):
+    *arrays, out_ref = refs
+    heads, _, _, width = out_ref.shape
+    for kind, array in enumerate(arrays):
+        for h in range(heads):
+            out_ref[h, kind] = array[:, h * width : (h + 1) * width]
+
+
+def unpack_kernel(back_ref, *refs):
+    heads, kinds, _, width = back_ref.shape
+    for kind, out in enumerate(refs[len(refs) - kinds :]):
+        for h in range(heads):
+            out[:, h * width : (h + 1) * width] = back_ref[h, kind]
+
+
 def whole():
     return pl.BlockSpec(memory_space=pltpu.VMEM)
 
 
-def passed_along(array, axis, by):
-    devices = lax.axis_size(axis)
+SMEM = pl.BlockSpec(memory_space=pltpu.SMEM)
+PARAMS = pltpu.CompilerParams(vmem_limit_bytes=40 * 1024 * 1024)
+PACK_PARAMS = pltpu.CompilerParams(vmem_limit_bytes=60 * 1024 * 1024)
+STEP = 4
+
+
+def packed(arrays, half, heads):
+    rows, columns = arrays[0].shape
+    width = columns // (PHASES * heads)
+    steps = heads // STEP
+    return pl.pallas_call(
+        pack_kernel,
+        grid=(steps,),
+        out_shape=jax.ShapeDtypeStruct((heads, len(arrays), rows, width), BF16),
+        in_specs=[pl.BlockSpec((rows, STEP * width), lambda i: (0, half * steps + i))] * len(arrays),
+        out_specs=pl.BlockSpec((STEP, len(arrays), rows, width), lambda i: (i, 0, 0, 0)),
+        compiler_params=PACK_PARAMS,
+        cost_estimate=pl.CostEstimate(flops=0, bytes_accessed=4 << 20, transcendentals=0),
+        name="pack",
+    )(*arrays)
+
+
+def unpacked(back, half, before):
+    heads, kinds, rows, width = back.shape
+    steps = heads // STEP
+    shape = jax.ShapeDtypeStruct((rows, PHASES * heads * width), BF16)
+    return pl.pallas_call(
+        unpack_kernel,
+        grid=(steps,),
+        out_shape=(shape,) * kinds,
+        in_specs=[pl.BlockSpec((STEP, kinds, rows, width), lambda i: (i, 0, 0, 0))]
+        + [pl.BlockSpec(memory_space=pl.ANY)] * len(before),
+        out_specs=(pl.BlockSpec((rows, STEP * width), lambda i: (0, half * steps + i)),) * kinds,
+        input_output_aliases={1 + i: i for i in range(len(before))},
+        compiler_params=PARAMS,
+        cost_estimate=pl.CostEstimate(flops=0, bytes_accessed=3 << 20, transcendentals=0),
+        name="unpack",
+    )(back, *before)
+
+
+def passed_along(array, by):
+    devices = lax.axis_size(("blk", "uly"))
     pairs = [(i, i + by) for i in range(devices) if 0 <= i + by < devices]
-    return lax.ppermute(array, axis, pairs)
-
-
-def body(queries, keys, values, grad_out, doc_start):
-    ulys = lax.axis_size("uly")
-    rows, columns = queries.shape
-    width = columns // ulys
-    blocks = ulys * rows // BLOCK
-    group = lax.axis_index("blk")
-    last = lax.axis_size("blk") - 1
-
-    packed = jnp.stack(
-        [a.reshape(rows, ulys, width) for a in (queries, grad_out, keys, values)], 0
-    ).transpose(2, 0, 1, 3)
-    x = lax.all_to_all(packed, "uly", split_axis=0, concat_axis=0, tiled=True)
-
-    own = lax.dynamic_slice_in_dim(doc_start, group * blocks, blocks, 0) // BLOCK - group * blocks
-    after = lax.dynamic_slice_in_dim(doc_start, jnp.minimum(group + 1, last) * blocks, 1, 0) // BLOCK
-    after = jnp.where(group == last, EDGE, after - group * blocks - (blocks - EDGE))
-    starts = jnp.concatenate([own, after]).astype(jnp.int32)
-
-    far = passed_along(x[blocks - REACH :, KEY : VALUE + 1], "blk", 1)
-    near = passed_along(x[:REACH, QUERY : DOUT + 1], "blk", -1)
-
-    smem = pl.BlockSpec(memory_space=pltpu.SMEM)
-    params = pltpu.CompilerParams(vmem_limit_bytes=48 * 1024 * 1024)
-    tile_shape = (BLOCK, width)
+    return lax.ppermute(array, ("blk", "uly"), pairs)
+
+
+def head_grads(starts, x, heads):
+    blocks = x.shape[0]
+    tile_shape = x.shape[2:]
+    far = passed_along(x[blocks - REACH :, KEY : VALUE + 1], heads)
+    near = passed_along(x[:REACH, QUERY : DOUT + 1], -heads)
     out_type = jax.ShapeDtypeStruct((blocks, 3) + tile_shape, BF16)
     edge_type = jax.ShapeDtypeStruct((EDGE, 2) + tile_shape, F32)
     out, head_acc, tail_acc = pl.pallas_call(
         inner_kernel,
         out_shape=(out_type, edge_type, edge_type),
-        in_specs=[smem, whole()],
+        in_specs=[SMEM, whole()],
         out_specs=(whole(), whole(), whole()),
         scratch_shapes=[pltpu.VMEM((blocks,) + tile_shape, F32)] * 2,
-        compiler_params=params,
-        cost_estimate=pl.CostEstimate(
-            flops=10 * 120 * BLOCK**3 * 4, bytes_accessed=9 << 20, transcendentals=120 << 14
-        ),
+        compiler_params=PARAMS,
+        cost_estimate=pl.CostEstimate(flops=8 * 10**9, bytes_accessed=6 << 20, transcendentals=1 << 20),
         name="inner",
     )(starts, x)
 
@@ -239,7 +273,7 @@
         grid=(1,),
         out_shape=(out_type, jax.ShapeDtypeStruct(stat_shape, F32)),
         in_specs=[
-            smem,
+            SMEM,
             edge_in(4, 0),
             full((REACH, 2) + tile_shape),
             full((EDGE, 2) + tile_shape),
@@ -249,17 +283,18 @@
         scratch_shapes=[pltpu.VMEM((REACH + EDGE,) + tile_shape, BF16)] * 2
         + [pltpu.VMEM((REACH + EDGE,) + tile_shape, F32)] * 2,
         input_output_aliases={4: 0},
-        compiler_params=params,
+        compiler_params=PARAMS,
+        cost_estimate=pl.CostEstimate(flops=2 * 10**9, bytes_accessed=3 << 20, transcendentals=1 << 18),
         name="head",
     )(starts, x, far, head_acc, out)
-    stats = passed_along(stats, "blk", -1)
+    stats = passed_along(stats, -heads)
     at_end = blocks // EDGE - 1
-    out = pl.pallas_call(
+    return pl.pallas_call(
         tail_kernel,
         grid=(1,),
         out_shape=out_type,
         in_specs=[
-            smem,
+            SMEM,
             edge_in(4, at_end),
             full((REACH, 2) + tile_shape),
             full(stat_shape),
@@ -269,13 +304,40 @@
         out_specs=edge_in(2, at_end),
         scratch_shapes=[pltpu.VMEM((EDGE,) + tile_shape, F32)] * 2,
         input_output_aliases={5: 0},
-        compiler_params=params,
+        compiler_params=PARAMS,
+        cost_estimate=pl.CostEstimate(flops=2 * 10**9, bytes_accessed=3 << 20, transcendentals=1 << 18),
         name="tail",
     )(starts, x, near, stats, tail_acc, out)
 
-    back = lax.all_to_all(out, "uly", split_axis=0, concat_axis=0, tiled=True)
-    back = back.transpose(1, 2, 0, 3).reshape(3, rows, columns)
-    return back[GQUERY], back[GKEY], back[GVALUE]
+
+PHASES = 2
+
+
+def body(queries, keys, values, grad_out, doc_start):
+    ulys = lax.axis_size("uly")
+    heads = ulys // PHASES
+    groups = [list(range(g * heads, (g + 1) * heads)) for g in range(PHASES)]
+
+    blocks = heads * queries.shape[0] // BLOCK
+    segment = lax.axis_index("blk") * PHASES + lax.axis_index("uly") // heads
+    last = lax.axis_size("blk") * PHASES - 1
+    own = lax.dynamic_slice_in_dim(doc_start, segment * blocks, blocks, 0) // BLOCK - segment * blocks
+    after = lax.dynamic_slice_in_dim(doc_start, jnp.minimum(segment + 1, last) * blocks, 1, 0) // BLOCK
+    after = jnp.where(segment == last, EDGE, after - segment * blocks - (blocks - EDGE))
+    starts = jnp.concatenate([own, after]).astype(jnp.int32)
+
+    def exchanged(array):
+        return lax.all_to_all(
+            array, "uly", split_axis=0, concat_axis=0, tiled=True, axis_index_groups=groups
+        )
+
+    arrays = (queries, grad_out, keys, values)
+    inputs = [exchanged(packed(arrays, p, heads)) for p in range(PHASES)]
+    grads = [exchanged(head_grads(starts, x, heads)) for x in inputs]
+    outs = ()
+    for p in range(PHASES):
+        outs = unpacked(grads[p], p, outs)
+    return outs[GQUERY], outs[GKEY], outs[GVALUE]
 
 
 def solution(mesh):

time: 249 us -> 216 us (0.87)
  blocking collectives: 82.6 us -> 0 us
  starting transfers between devices: 20.1 us -> 47.6 us
  waiting for transfers between devices: 93.4 us -> 117 us
  Pallas kernels: 22.3 us -> 36.3 us
  local copies, waits for them, and re-layouts: 20.4 us -> 8.3 us
  other arithmetic: 3.6 us -> 0.16 us
    all_to_all x1 -> x0, blocking collectives: 82.6 us -> none  [body(): back = lax.all_to_all(out, 'uly', split_axis=0, concat_axis=0, tiled=True)]
    ppermute x3 -> x6, waiting for transfers between devices: 3.27 us -> 32 us  [passed_along(): return lax.ppermute(array, ('blk', 'uly'), pairs)]
    all_to_all x1 -> x4, starting transfers between devices: 12.1 us -> 28.4 us  [exchanged(): lax.all_to_all(array, 'uly', split_axis=0, concat_axis=0, tiled=True, axi...]
    pallas_call x3 -> x10, Pallas kernels: 22.3 us -> 36.3 us  [the longest x2 11.4 us: head_grads(): pl.pallas_call(inner_kernel, out_shape=(out_type, edge_type, edge_type),...]
    ppermute x3 -> x6, starting transfers between devices: 8.05 us -> 19.2 us  [passed_along(): return lax.ppermute(array, ('blk', 'uly'), pairs)]
    unnamed x9 -> x10, local copies, waits for them, and re-layouts: 10.4 us -> 5.22 us
    all_to_all x1 -> x4, waiting for transfers between devices: 90.1 us -> 85.1 us  [exchanged(): lax.all_to_all(array, 'uly', split_axis=0, concat_axis=0, tiled=True, axi...]
    another operation x4 -> x0, local copies, waits for them, and re-layouts: 3.95 us -> none  [body(): jnp.stack([a.reshape(rows, ulys, width) for a in (queries, grad_out, keys...]
  transfers between devices with their start and end apart: 4 -> 10, of which waited for: 2 -> 7; matrix products, arithmetic and copies ran while one was open for 0% -> 2% of each run, Pallas kernels for 7% -> 14%
where the time goes in v2:
time: 216 us; the launch traced here: 213 us
  waiting for transfers between devices  117 us (54%)
  starting transfers between devices  47.6 us (22%)
  Pallas kernels  36.3 us (17%)
  local copies, waits for them, and re-layouts  8.3 us (4%)
  between operations  3.42 us (2%)
    all_to_all x4, waiting for transfers between devices, exchanged(): lax.all_to_all(array, 'uly', split_axis=0, concat_axis=0, tiled=True, axi...  85.1 us
    ppermute x6, waiting for transfers between devices, passed_along(): return lax.ppermute(array, ('blk', 'uly'), pairs)  32 us
    all_to_all x4, starting transfers between devices, exchanged(): lax.all_to_all(array, 'uly', split_axis=0, concat_axis=0, tiled=True, axi...  28.4 us
    ppermute x6, starting transfers between devices, passed_along(): return lax.ppermute(array, ('blk', 'uly'), pairs)  19.2 us
    pallas_call x2, Pallas kernels, head_grads(): pl.pallas_call(inner_kernel, out_shape=(out_type, edge_type, edge_type),...  11.4 us
    pallas_call x2, Pallas kernels, head_grads(): pl.pallas_call(head_kernel, grid=(1,), out_shape=(out_type, jax.ShapeDtyp...  8.76 us
    pallas_call x2, Pallas kernels, packed(): pl.pallas_call(pack_kernel, grid=(steps,), out_shape=jax.ShapeDtypeStruct...  7.93 us
    unnamed x10, local copies, waits for them, and re-layouts  5.22 us
  transfers between devices with their start and end apart: 10, of which 7 were waited for; matrix products, arithmetic and copies ran while one was open for 2% of the time, Pallas kernels for 14%

profile of v2, /device:TPU:23, one launch (start us, length us, event | category | flops | bytes accessed | tf_op | source)
XLA Modules:
  0.0 212.9 jit_solution(9017293328406901916)
XLA Ops:
  0.6 4.0 %pack.3 = bf16[16,4,128,128]{3,2,1,0:T(8,128)(2,1)} custom-call(bf16[128,4096]{1,0:T(8,128)(2,1)} %refs_0_.3, bf16[128,4096]{1,0:T(8,128)(2,1)} %refs_1_.3, bf16[128,4096]{1,0:T(8,128)(2,1)} %refs_2_.3, bf16[128,4096]{1,0:T(8,128)(2,1)} %refs_3_.3), custom_call_target="tpu_custom_call" | custom-call | bytes 4194304 | tf_op jit(solution)/shard_map/pack/pallas_call | solution.py:210
  4.6 9.2 %all-to-all-start.2 = ((bf16[16,4,128,128]{3,2,1,0:T(8,128)(2,1)}), bf16[16,4,128,128]{3,2,1,0:T(8,128)(2,1)}, u32[]{:S(2)}, u32[]{:S(2)}) async-start(bf16[16,4,128,128]{3,2,1,0:T(8,128)(2,1)} %pack.3), calls=%async_computation.2 | async-start | bytes 4194304 | tf_op jit(solution)/shard_map/all_to_all | solution.py:330
  13.8 4.0 %pack.2 = bf16[16,4,128,128]{3,2,1,0:T(8,128)(2,1)} custom-call(bf16[128,4096]{1,0:T(8,128)(2,1)} %refs_0_.3, bf16[128,4096]{1,0:T(8,128)(2,1)} %refs_1_.3, bf16[128,4096]{1,0:T(8,128)(2,1)} %refs_2_.3, bf16[128,4096]{1,0:T(8,128)(2,1)} %refs_3_.3), custom_call_target="tpu_custom_call" | custom-call | bytes 4194304 | tf_op jit(solution)/shard_map/pack/pallas_call | solution.py:210
  17.7 45.1 %all-to-all-done.2.x_ref = bf16[16,4,128,128]{3,2,1,0:T(8,128)(2,1)} async-done(((bf16[16,4,128,128]{3,2,1,0:T(8,128)(2,1)}), bf16[16,4,128,128]{3,2,1,0:T(8,128)(2,1)}, u32[]{:S(2)}, u32[]{:S(2)}) %all-to-all-start.2) | async-done | bytes 2097184 | tf_op jit(solution)/shard_map/all_to_all | solution.py:330
  62.8 5.0 %all-to-all-start = ((bf16[16,4,128,128]{3,2,1,0:T(8,128)(2,1)}), bf16[16,4,128,128]{3,2,1,0:T(8,128)(2,1)S(1)}, u32[]{:S(2)}, u32[]{:S(2)}) async-start(bf16[16,4,128,128]{3,2,1,0:T(8,128)(2,1)} %pack.2), calls=%async_computation | async-start | bytes 4194304 | tf_op jit(solution)/shard_map/all_to_all | solution.py:330
  72.4 3.0 %collective-permute-start.3 = (bf16[7,2,128,128]{3,2,1,0:T(8,128)(2,1)S(1)}, bf16[7,2,128,128]{3,2,1,0:T(8,128)(2,1)S(1)}, u32[]{:S(2)}, u32[]{:S(2)}) collective-permute-start(bf16[7,2,128,128]{3,2,1,0:T(8,128)(2,1)S(1)} %get-tuple-element.36), channel_id=1, source_target_pairs={{16,0},{17,1},{18,2},{19,3},{20,4},{21,5},{22,6},{23,7},{24,8},{25... | collective-permute-start | bytes 1376264 | tf_op jit(solution)/shard_map/ppermute | solution.py:243
  75.5 4.7 %collective-permute-start.4 = (bf16[7,2,128,128]{3,2,1,0:T(8,128)(2,1)S(1)}, bf16[7,2,128,128]{3,2,1,0:T(8,128)(2,1)S(1)}, u32[]{:S(2)}, u32[]{:S(2)}) collective-permute-start(bf16[7,2,128,128]{3,2,1,0:T(8,128)(2,1)S(1)} %get-tuple-element.35), channel_id=1, source_target_pairs={{0,16},{1,17},{2,18},{3,19},{4,20},{5,21},{6,22},{7,23},{8,24},{9,... | collective-permute-start | bytes 1376264 | tf_op jit(solution)/shard_map/ppermute | solution.py:243
  80.1 6.1 %inner.3 = (bf16[16,3,128,128]{3,2,1,0:T(8,128)(2,1)S(1)}, f32[8,2,128,128]{3,2,1,0:T(8,128)S(1)}, f32[8,2,128,128]{3,2,1,0:T(8,128)S(1)}) custom-call(s32[17]{0:T(128)S(1)} %pad_add_fusion.st_ref, bf16[16,4,128,128]{3,2,1,0:T(8,128)(2,1)} %all-to-all-done.2.x_ref), custom_call_target="tpu_custom_call" | custom-call | flops 8000000000 | bytes 6291456 | tf_op jit(solution)/shard_map/inner/pallas_call | solution.py:253
  86.2 11.3 %collective-permute-done.4.far_ref = bf16[7,2,128,128]{3,2,1,0:T(8,128)(2,1)S(1)} collective-permute-done((bf16[7,2,128,128]{3,2,1,0:T(8,128)(2,1)S(1)}, bf16[7,2,128,128]{3,2,1,0:T(8,128)(2,1)S(1)}, u32[]{:S(2)}, u32[]{:S(2)}) %collective-permute-start.4) | collective-permute-done | bytes 458784 | tf_op jit(solution)/shard_map/ppermute | solution.py:243
  97.5 4.7 %head.3 = (bf16[16,3,128,128]{3,2,1,0:T(8,128)(2,1)S(1)}, f32[4,8,256]{2,1,0:T(8,128)S(1)}) custom-call(s32[17]{0:T(128)S(1)} %pad_add_fusion.st_ref, bf16[16,4,128,128]{3,2,1,0:T(8,128)(2,1)} %all-to-all-done.2.x_ref, bf16[7,2,128,128]{3,2,1,0:T(8,128)(2,1)S(1)} %collective-permute-done.4.far_ref, ...), custom_call_target="tpu_custom_call", output_to_operand_aliasing={{0}: (4, {})} | custom-call | flops 2000000000 | bytes 3145728 | tf_op jit(solution)/shard_map/head/pallas_call | solution.py:271
  104.2 5.4 %collective-permute-done.5.stat_ref = f32[4,8,256]{2,1,0:T(8,128)S(1)} collective-permute-done((f32[4,8,256]{2,1,0:T(8,128)S(1)}, f32[4,8,256]{2,1,0:T(8,128)S(1)}, u32[]{:S(2)}, u32[]{:S(2)}) %collective-permute-start.5) | collective-permute-done | bytes 32800 | tf_op jit(solution)/shard_map/ppermute | solution.py:243
  109.6 2.7 %tail.3 = bf16[16,3,128,128]{3,2,1,0:T(8,128)(2,1)S(1)} custom-call(s32[17]{0:T(128)S(1)} %pad_add_fusion.st_ref, bf16[16,4,128,128]{3,2,1,0:T(8,128)(2,1)} %all-to-all-done.2.x_ref, bf16[7,2,128,128]{3,2,1,0:T(8,128)(2,1)S(1)} %collective-permute-done.3.near_ref, f32[4,8,256]{2,1,0:T(8,128)S(1)} %collective-permute-done.5.stat_ref, ...), custom_call_target="tpu_custom_call", output_to_operand_aliasing={{}: (5, {})} | custom-call | flops 2000000000 | bytes 3145728 | tf_op jit(solution)/shard_map/tail/pallas_call | solution.py:292
  113.4 3.3 %all-to-all-done.x_ref = bf16[16,4,128,128]{3,2,1,0:T(8,128)(2,1)S(1)} async-done(((bf16[16,4,128,128]{3,2,1,0:T(8,128)(2,1)}), bf16[16,4,128,128]{3,2,1,0:T(8,128)(2,1)S(1)}, u32[]{:S(2)}, u32[]{:S(2)}) %all-to-all-start) | async-done | bytes 2097184 | tf_op jit(solution)/shard_map/all_to_all | solution.py:330
  118.1 5.4 %all-to-all-start.3 = ((bf16[16,3,128,128]{3,2,1,0:T(8,128)(2,1)}), bf16[16,3,128,128]{3,2,1,0:T(8,128)(2,1)S(1)}, u32[]{:S(2)}, u32[]{:S(2)}) async-start(bf16[16,3,128,128]{3,2,1,0:T(8,128)(2,1)} %copy-done.2), calls=%async_computation.3 | async-start | bytes 3145728 | tf_op jit(solution)/shard_map/all_to_all | solution.py:330
  124.7 2.7 %collective-permute-start = (bf16[7,2,128,128]{3,2,1,0:T(8,128)(2,1)S(1)}, bf16[7,2,128,128]{3,2,1,0:T(8,128)(2,1)S(1)}, u32[]{:S(2)}, u32[]{:S(2)}) collective-permute-start(bf16[7,2,128,128]{3,2,1,0:T(8,128)(2,1)S(1)} %get-tuple-element.38), channel_id=1, source_target_pairs={{16,0},{17,1},{18,2},{19,3},{20,4},{21,5},{22,6},{23,7},{24,8},{25... | collective-permute-start | bytes 1376264 | tf_op jit(solution)/shard_map/ppermute | solution.py:243
  127.4 5.0 %collective-permute-start.1 = (bf16[7,2,128,128]{3,2,1,0:T(8,128)(2,1)S(1)}, bf16[7,2,128,128]{3,2,1,0:T(8,128)(2,1)S(1)}, u32[]{:S(2)}, u32[]{:S(2)}) collective-permute-start(bf16[7,2,128,128]{3,2,1,0:T(8,128)(2,1)S(1)} %get-tuple-element.37), channel_id=1, source_target_pairs={{0,16},{1,17},{2,18},{3,19},{4,20},{5,21},{6,22},{7,23},{8,24},{9,... | collective-permute-start | bytes 1376264 | tf_op jit(solution)/shard_map/ppermute | solution.py:243
  134.0 5.3 %inner.2 = (bf16[16,3,128,128]{3,2,1,0:T(8,128)(2,1)S(1)}, f32[8,2,128,128]{3,2,1,0:T(8,128)S(1)}, f32[8,2,128,128]{3,2,1,0:T(8,128)S(1)}) custom-call(s32[17]{0:T(128)S(1)} %pad_add_fusion.st_ref, bf16[16,4,128,128]{3,2,1,0:T(8,128)(2,1)S(1)} %copy-done.1), custom_call_target="tpu_custom_call" | custom-call | flops 8000000000 | bytes 6291456 | tf_op jit(solution)/shard_map/inner/pallas_call | solution.py:253
  139.3 10.2 %collective-permute-done.1.far_ref = bf16[7,2,128,128]{3,2,1,0:T(8,128)(2,1)S(1)} collective-permute-done((bf16[7,2,128,128]{3,2,1,0:T(8,128)(2,1)S(1)}, bf16[7,2,128,128]{3,2,1,0:T(8,128)(2,1)S(1)}, u32[]{:S(2)}, u32[]{:S(2)}) %collective-permute-start.1) | collective-permute-done | bytes 458784 | tf_op jit(solution)/shard_map/ppermute | solution.py:243
  149.5 4.1 %head.2 = (bf16[16,3,128,128]{3,2,1,0:T(8,128)(2,1)S(1)}, f32[4,8,256]{2,1,0:T(8,128)S(1)}) custom-call(s32[17]{0:T(128)S(1)} %pad_add_fusion.st_ref, bf16[16,4,128,128]{3,2,1,0:T(8,128)(2,1)S(1)} %copy-done.1, bf16[7,2,128,128]{3,2,1,0:T(8,128)(2,1)S(1)} %collective-permute-done.1.far_ref, ...), custom_call_target="tpu_custom_call", output_to_operand_aliasing={{0}: (4, {})} | custom-call | flops 2000000000 | bytes 3145728 | tf_op jit(solution)/shard_map/head/pallas_call | solution.py:271
  153.6 1.9 collective-permute-start.2
  155.5 5.1 %collective-permute-done.2.stat_ref = f32[4,8,256]{2,1,0:T(8,128)S(1)} collective-permute-done((f32[4,8,256]{2,1,0:T(8,128)S(1)}, f32[4,8,256]{2,1,0:T(8,128)S(1)}, u32[]{:S(2)}, u32[]{:S(2)}) %collective-permute-start.2) | collective-permute-done | bytes 32800 | tf_op jit(solution)/shard_map/ppermute | solution.py:243
  160.6 2.0 tail.2
  163.9 8.9 %all-to-all-start.1 = ((bf16[16,3,128,128]{3,2,1,0:T(8,128)(2,1)}), bf16[16,3,128,128]{3,2,1,0:T(8,128)(2,1)S(1)}, u32[]{:S(2)}, u32[]{:S(2)}) async-start(bf16[16,3,128,128]{3,2,1,0:T(8,128)(2,1)} %copy-done.3), calls=%async_computation.1 | async-start | bytes 3145728 | tf_op jit(solution)/shard_map/all_to_all | solution.py:330
  174.5 36.7 %all-to-all-done.1.back_ref = bf16[16,3,128,128]{3,2,1,0:T(8,128)(2,1)S(1)} async-done(((bf16[16,3,128,128]{3,2,1,0:T(8,128)(2,1)}), bf16[16,3,128,128]{3,2,1,0:T(8,128)(2,1)S(1)}, u32[]{:S(2)}, u32[]{:S(2)}) %all-to-all-start.1) | async-done | bytes 1572896 | tf_op jit(solution)/shard_map/all_to_all | solution.py:330
  (21 shorter events, 13.9 us)
Async XLA Ops:
  4.6 58.2 %all-to-all-start.2 = ((bf16[16,4,128,128]{3,2,1,0:T(8,128)(2,1)}), bf16[16,4,128,128]{3,2,1,0:T(8,128)(2,1)}, u32[]{:S(2)}, u32[]{:S(2)}) async-start(bf16[16,4,128,128]{3,2,1,0:T(8,128)(2,1)} %pack.3), calls=%async_computation.2 | async-start | bytes 4194304 | tf_op jit(solution)/shard_map/all_to_all | solution.py:330
  17.7 50.1 %copy-start.4 = (s32[256]{0:T(256)S(1)}, s32[256]{0:T(256)}, u32[]{:S(2)}) copy-start(s32[256]{0:T(256)} %param.9) | copy-start | bytes 3076
  62.8 53.9 %all-to-all-start = ((bf16[16,4,128,128]{3,2,1,0:T(8,128)(2,1)}), bf16[16,4,128,128]{3,2,1,0:T(8,128)(2,1)S(1)}, u32[]{:S(2)}, u32[]{:S(2)}) async-start(bf16[16,4,128,128]{3,2,1,0:T(8,128)(2,1)} %pack.2), calls=%async_computation | async-start | bytes 4194304 | tf_op jit(solution)/shard_map/all_to_all | solution.py:330
  72.4 31.7 %collective-permute-start.3 = (bf16[7,2,128,128]{3,2,1,0:T(8,128)(2,1)S(1)}, bf16[7,2,128,128]{3,2,1,0:T(8,128)(2,1)S(1)}, u32[]{:S(2)}, u32[]{:S(2)}) collective-permute-start(bf16[7,2,128,128]{3,2,1,0:T(8,128)(2,1)S(1)} %get-tuple-element.36), channel_id=1, source_target_pairs={{16,0},{17,1},{18,2},{19,3},{20,4},{21,5},{22,6},{23,7},{24,8},{25... | collective-permute-start | bytes 1376264 | tf_op jit(solution)/shard_map/ppermute | solution.py:243
  75.5 22.1 %collective-permute-start.4 = (bf16[7,2,128,128]{3,2,1,0:T(8,128)(2,1)S(1)}, bf16[7,2,128,128]{3,2,1,0:T(8,128)(2,1)S(1)}, u32[]{:S(2)}, u32[]{:S(2)}) collective-permute-start(bf16[7,2,128,128]{3,2,1,0:T(8,128)(2,1)S(1)} %get-tuple-element.35), channel_id=1, source_target_pairs={{0,16},{1,17},{2,18},{3,19},{4,20},{5,21},{6,22},{7,23},{8,24},{9,... | collective-permute-start | bytes 1376264 | tf_op jit(solution)/shard_map/ppermute | solution.py:243
  102.2 7.4 %collective-permute-start.5 = (f32[4,8,256]{2,1,0:T(8,128)S(1)}, f32[4,8,256]{2,1,0:T(8,128)S(1)}, u32[]{:S(2)}, u32[]{:S(2)}) collective-permute-start(f32[4,8,256]{2,1,0:T(8,128)S(1)} %get-tuple-element.26), channel_id=1, source_target_pairs={{16,0},{17,1},{18,2},{19,3},{20,4},{21,5},{22,6},{23,7},{24,8},{25... | collective-permute-start | bytes 98312 | tf_op jit(solution)/shard_map/ppermute | solution.py:243
  112.3 1.1 copy-start.2
  116.7 1.3 copy-start
  118.1 45.8 %all-to-all-start.3 = ((bf16[16,3,128,128]{3,2,1,0:T(8,128)(2,1)}), bf16[16,3,128,128]{3,2,1,0:T(8,128)(2,1)S(1)}, u32[]{:S(2)}, u32[]{:S(2)}) async-start(bf16[16,3,128,128]{3,2,1,0:T(8,128)(2,1)} %copy-done.2), calls=%async_computation.3 | async-start | bytes 3145728 | tf_op jit(solution)/shard_map/all_to_all | solution.py:330
  124.7 30.8 %collective-permute-start = (bf16[7,2,128,128]{3,2,1,0:T(8,128)(2,1)S(1)}, bf16[7,2,128,128]{3,2,1,0:T(8,128)(2,1)S(1)}, u32[]{:S(2)}, u32[]{:S(2)}) collective-permute-start(bf16[7,2,128,128]{3,2,1,0:T(8,128)(2,1)S(1)} %get-tuple-element.38), channel_id=1, source_target_pairs={{16,0},{17,1},{18,2},{19,3},{20,4},{21,5},{22,6},{23,7},{24,8},{25... | collective-permute-start | bytes 1376264 | tf_op jit(solution)/shard_map/ppermute | solution.py:243
  127.4 22.1 %collective-permute-start.1 = (bf16[7,2,128,128]{3,2,1,0:T(8,128)(2,1)S(1)}, bf16[7,2,128,128]{3,2,1,0:T(8,128)(2,1)S(1)}, u32[]{:S(2)}, u32[]{:S(2)}) collective-permute-start(bf16[7,2,128,128]{3,2,1,0:T(8,128)(2,1)S(1)} %get-tuple-element.37), channel_id=1, source_target_pairs={{0,16},{1,17},{2,18},{3,19},{4,20},{5,21},{6,22},{7,23},{8,24},{9,... | collective-permute-start | bytes 1376264 | tf_op jit(solution)/shard_map/ppermute | solution.py:243
  132.4 1.6 copy-start.1
  153.6 7.1 %collective-permute-start.2 = (f32[4,8,256]{2,1,0:T(8,128)S(1)}, f32[4,8,256]{2,1,0:T(8,128)S(1)}, u32[]{:S(2)}, u32[]{:S(2)}) collective-permute-start(f32[4,8,256]{2,1,0:T(8,128)S(1)} %get-tuple-element.21), channel_id=1, source_target_pairs={{16,0},{17,1},{18,2},{19,3},{20,4},{21,5},{22,6},{23,7},{24,8},{25... | collective-permute-start | bytes 98312 | tf_op jit(solution)/shard_map/ppermute | solution.py:243
  162.7 1.2 copy-start.3
  163.9 47.3 %all-to-all-start.1 = ((bf16[16,3,128,128]{3,2,1,0:T(8,128)(2,1)}), bf16[16,3,128,128]{3,2,1,0:T(8,128)(2,1)S(1)}, u32[]{:S(2)}, u32[]{:S(2)}) async-start(bf16[16,3,128,128]{3,2,1,0:T(8,128)(2,1)} %copy-done.3), calls=%async_computation.1 | async-start | bytes 3145728 | tf_op jit(solution)/shard_map/all_to_all | solution.py:330

commit v3 on v2

--- a/solution.py
+++ b/solution.py
@@ -58,11 +58,12 @@
     return gq, gk, gv, lse, delta
 
 
-def inner_kernel(st_ref, x_ref, out_ref, head_ref, tail_ref, gk_ref, gv_ref):
+def inner_kernel(st_ref, x_ref, out_ref, head_ref, tail_ref, near_ref, gk_ref, gv_ref):
     blocks = x_ref.shape[0]
     width = x_ref.shape[-1]
     gk_ref[...] = jnp.zeros_like(gk_ref)
     gv_ref[...] = jnp.zeros_like(gv_ref)
+    near_ref[...] = x_ref[:REACH, QUERY : DOUT + 1]
 
     def tile(t, _):
         first = st_ref[2 * t]
@@ -200,7 +201,7 @@
 SMEM = pl.BlockSpec(memory_space=pltpu.SMEM)
 PARAMS = pltpu.CompilerParams(vmem_limit_bytes=40 * 1024 * 1024)
 PACK_PARAMS = pltpu.CompilerParams(vmem_limit_bytes=60 * 1024 * 1024)
-STEP = 4
+STEP = 16
 
 
 def packed(arrays, half, heads):
@@ -247,14 +248,14 @@
     blocks = x.shape[0]
     tile_shape = x.shape[2:]
     far = passed_along(x[blocks - REACH :, KEY : VALUE + 1], heads)
-    near = passed_along(x[:REACH, QUERY : DOUT + 1], -heads)
     out_type = jax.ShapeDtypeStruct((blocks, 3) + tile_shape, BF16)
     edge_type = jax.ShapeDtypeStruct((EDGE, 2) + tile_shape, F32)
-    out, head_acc, tail_acc = pl.pallas_call(
+    near_type = jax.ShapeDtypeStruct((REACH, 2) + tile_shape, BF16)
+    out, head_acc, tail_acc, near = pl.pallas_call(
         inner_kernel,
-        out_shape=(out_type, edge_type, edge_type),
+        out_shape=(out_type, edge_type, edge_type, near_type),
         in_specs=[SMEM, whole()],
-        out_specs=(whole(), whole(), whole()),
+        out_specs=(whole(),) * 4,
         scratch_shapes=[pltpu.VMEM((blocks,) + tile_shape, F32)] * 2,
         compiler_params=PARAMS,
         cost_estimate=pl.CostEstimate(flops=8 * 10**9, bytes_accessed=6 << 20, transcendentals=1 << 20),
@@ -288,6 +289,7 @@
         name="head",
     )(starts, x, far, head_acc, out)
     stats = passed_along(stats, -heads)
+    near = passed_along(near, -heads)
     at_end = blocks // EDGE - 1
     return pl.pallas_call(
         tail_kernel,

time: 216 us -> 207 us (0.958)
  Pallas kernels: 36.3 us -> 32.1 us
  starting transfers between devices: 47.6 us -> 44.9 us
    ppermute x6, waiting for transfers between devices: 32 us -> 16.9 us  [passed_along(): return lax.ppermute(array, ('blk', 'uly'), pairs)]
    all_to_all x4, waiting for transfers between devices: 85.1 us -> 99.6 us  [exchanged(): lax.all_to_all(array, 'uly', split_axis=0, concat_axis=0, tiled=True, axi...]
    pallas_call x2, Pallas kernels: 8.76 us -> 2.64 us  [head_grads(): pl.pallas_call(head_kernel, grid=(1,), out_shape=(out_type, jax.ShapeDtyp...]
    all_to_all x4, starting transfers between devices: 28.4 us -> 23.4 us  [exchanged(): lax.all_to_all(array, 'uly', split_axis=0, concat_axis=0, tiled=True, axi...]
    pallas_call x2, Pallas kernels: 11.4 us -> 16 us  [head_grads(): pl.pallas_call(inner_kernel, out_shape=(out_type, edge_type, edge_type, n...]
    ppermute x6, starting transfers between devices: 19.2 us -> 21.5 us  [passed_along(): return lax.ppermute(array, ('blk', 'uly'), pairs)]
  transfers between devices with their start and end apart: 10 -> 10, of which waited for: 7 -> 10; matrix products, arithmetic and copies ran while one was open for 2% -> 1% of each run, Pallas kernels for 14% -> 13%
where the time goes in v3:
time: 207 us; the launch traced here: 205 us
  waiting for transfers between devices  117 us (57%)
  starting transfers between devices  44.9 us (22%)
  Pallas kernels  32.1 us (16%)
  local copies, waits for them, and re-layouts  7.9 us (4%)
  between operations  3.4 us (2%)
    all_to_all x4, waiting for transfers between devices, exchanged(): lax.all_to_all(array, 'uly', split_axis=0, concat_axis=0, tiled=True, axi...  99.6 us
    all_to_all x4, starting transfers between devices, exchanged(): lax.all_to_all(array, 'uly', split_axis=0, concat_axis=0, tiled=True, axi...  23.4 us
    ppermute x6, starting transfers between devices, passed_along(): return lax.ppermute(array, ('blk', 'uly'), pairs)  21.5 us
    ppermute x6, waiting for transfers between devices, passed_along(): return lax.ppermute(array, ('blk', 'uly'), pairs)  16.9 us
    pallas_call x2, Pallas kernels, head_grads(): pl.pallas_call(inner_kernel, out_shape=(out_type, edge_type, edge_type, n...  16 us
    pallas_call x2, Pallas kernels, packed(): pl.pallas_call(pack_kernel, grid=(steps,), out_shape=jax.ShapeDtypeStruct...  6.43 us
    unnamed x10, local copies, waits for them, and re-layouts  5.21 us
  transfers between devices with their start and end apart: 10, of which 10 were waited for; matrix products, arithmetic and copies ran while one was open for 1% of the time, Pallas kernels for 13%

profile of v3, /device:TPU:23, one launch (start us, length us, event | category | flops | bytes accessed | tf_op | source)
XLA Modules:
  0.0 205.0 jit_solution(12027442699416494785)
XLA Ops:
  0.6 3.2 %pack.3 = bf16[16,4,128,128]{3,2,1,0:T(8,128)(2,1)} custom-call(bf16[128,4096]{1,0:T(8,128)(2,1)} %refs_0_.3, bf16[128,4096]{1,0:T(8,128)(2,1)} %refs_1_.3, bf16[128,4096]{1,0:T(8,128)(2,1)} %refs_2_.3, bf16[128,4096]{1,0:T(8,128)(2,1)} %refs_3_.3), custom_call_target="tpu_custom_call" | custom-call | bytes 4194304 | tf_op jit(solution)/shard_map/pack/pallas_call | solution.py:211
  3.8 9.2 %all-to-all-start.2 = ((bf16[16,4,128,128]{3,2,1,0:T(8,128)(2,1)}), bf16[16,4,128,128]{3,2,1,0:T(8,128)(2,1)}, u32[]{:S(2)}, u32[]{:S(2)}) async-start(bf16[16,4,128,128]{3,2,1,0:T(8,128)(2,1)} %pack.3), calls=%async_computation.2 | async-start | bytes 4194304 | tf_op jit(solution)/shard_map/all_to_all | solution.py:332
  13.0 3.2 %pack.2 = bf16[16,4,128,128]{3,2,1,0:T(8,128)(2,1)} custom-call(bf16[128,4096]{1,0:T(8,128)(2,1)} %refs_0_.3, bf16[128,4096]{1,0:T(8,128)(2,1)} %refs_1_.3, bf16[128,4096]{1,0:T(8,128)(2,1)} %refs_2_.3, bf16[128,4096]{1,0:T(8,128)(2,1)} %refs_3_.3), custom_call_target="tpu_custom_call" | custom-call | bytes 4194304 | tf_op jit(solution)/shard_map/pack/pallas_call | solution.py:211
  16.2 45.8 %all-to-all-done.2.x_ref = bf16[16,4,128,128]{3,2,1,0:T(8,128)(2,1)} async-done(((bf16[16,4,128,128]{3,2,1,0:T(8,128)(2,1)}), bf16[16,4,128,128]{3,2,1,0:T(8,128)(2,1)}, u32[]{:S(2)}, u32[]{:S(2)}) %all-to-all-start.2) | async-done | bytes 2097184 | tf_op jit(solution)/shard_map/all_to_all | solution.py:332
  62.1 5.0 %all-to-all-start = ((bf16[16,4,128,128]{3,2,1,0:T(8,128)(2,1)}), bf16[16,4,128,128]{3,2,1,0:T(8,128)(2,1)S(1)}, u32[]{:S(2)}, u32[]{:S(2)}) async-start(bf16[16,4,128,128]{3,2,1,0:T(8,128)(2,1)} %pack.2), calls=%async_computation | async-start | bytes 4194304 | tf_op jit(solution)/shard_map/all_to_all | solution.py:332
  71.5 3.8 %collective-permute-start.4 = (bf16[7,2,128,128]{3,2,1,0:T(8,128)(2,1)S(1)}, bf16[7,2,128,128]{3,2,1,0:T(8,128)(2,1)S(1)}, u32[]{:S(2)}, u32[]{:S(2)}) collective-permute-start(bf16[7,2,128,128]{3,2,1,0:T(8,128)(2,1)S(1)} %slice.9), channel_id=1, source_target_pairs={{0,16},{1,17},{2,18},{3,19},{4,20},{5,21},{6,22},{7,23},{8,24},{9,... | collective-permute-start | bytes 1376264 | tf_op jit(solution)/shard_map/ppermute | solution.py:244
  75.2 8.5 %inner.3 = (bf16[16,3,128,128]{3,2,1,0:T(8,128)(2,1)S(1)}, f32[8,2,128,128]{3,2,1,0:T(8,128)S(1)}, f32[8,2,128,128]{3,2,1,0:T(8,128)S(1)}, bf16[7,2,128,128]{3,2,1,0:T(8,128)(2,1)S(1)}) custom-call(s32[17]{0:T(128)S(1)} %pad_add_fusion.st_ref, bf16[16,4,128,128]{3,2,1,0:T(8,128)(2,1)} %all-to-all-done.2.x_ref), custom_call_target="tpu_custom_call" | custom-call | flops 8000000000 | bytes 6291456 | tf_op jit(solution)/shard_map/inner/pallas_call | solution.py:254
  83.8 2.1 %collective-permute-start.3 = (bf16[7,2,128,128]{3,2,1,0:T(8,128)(2,1)S(1)}, bf16[7,2,128,128]{3,2,1,0:T(8,128)(2,1)S(1)}, u32[]{:S(2)}, u32[]{:S(2)}) collective-permute-start(bf16[7,2,128,128]{3,2,1,0:T(8,128)(2,1)S(1)} %get-tuple-element.27), channel_id=1, source_target_pairs={{16,0},{17,1},{18,2},{19,3},{20,4},{21,5},{22,6},{23,7},{24,8},{25... | collective-permute-start | bytes 1376264 | tf_op jit(solution)/shard_map/ppermute | solution.py:244
  86.8 1.7 head.3
  88.5 4.8 %collective-permute-start.5 = (f32[4,8,256]{2,1,0:T(8,128)S(1)}, f32[4,8,256]{2,1,0:T(8,128)S(1)}, u32[]{:S(2)}, u32[]{:S(2)}) collective-permute-start(f32[4,8,256]{2,1,0:T(8,128)S(1)} %get-tuple-element.30), channel_id=1, source_target_pairs={{16,0},{17,1},{18,2},{19,3},{20,4},{21,5},{22,6},{23,7},{24,8},{25... | collective-permute-start | bytes 98312 | tf_op jit(solution)/shard_map/ppermute | solution.py:244
  93.3 6.5 %collective-permute-done.3.near_ref = bf16[7,2,128,128]{3,2,1,0:T(8,128)(2,1)S(1)} collective-permute-done((bf16[7,2,128,128]{3,2,1,0:T(8,128)(2,1)S(1)}, bf16[7,2,128,128]{3,2,1,0:T(8,128)(2,1)S(1)}, u32[]{:S(2)}, u32[]{:S(2)}) %collective-permute-start.3) | collective-permute-done | bytes 458784 | tf_op jit(solution)/shard_map/ppermute | solution.py:244
  100.4 2.3 %tail.3 = bf16[16,3,128,128]{3,2,1,0:T(8,128)(2,1)S(1)} custom-call(s32[17]{0:T(128)S(1)} %pad_add_fusion.st_ref, bf16[16,4,128,128]{3,2,1,0:T(8,128)(2,1)} %all-to-all-done.2.x_ref, bf16[7,2,128,128]{3,2,1,0:T(8,128)(2,1)S(1)} %collective-permute-done.3.near_ref, f32[4,8,256]{2,1,0:T(8,128)S(1)} %collective-permute-done.5.stat_ref, ...), custom_call_target="tpu_custom_call", output_to_operand_aliasing={{}: (5, {})} | custom-call | flops 2000000000 | bytes 3145728 | tf_op jit(solution)/shard_map/tail/pallas_call | solution.py:294
  103.9 12.1 %all-to-all-done.x_ref = bf16[16,4,128,128]{3,2,1,0:T(8,128)(2,1)S(1)} async-done(((bf16[16,4,128,128]{3,2,1,0:T(8,128)(2,1)}), bf16[16,4,128,128]{3,2,1,0:T(8,128)(2,1)S(1)}, u32[]{:S(2)}, u32[]{:S(2)}) %all-to-all-start) | async-done | bytes 2097184 | tf_op jit(solution)/shard_map/all_to_all | solution.py:332
  117.3 5.0 %all-to-all-start.3 = ((bf16[16,3,128,128]{3,2,1,0:T(8,128)(2,1)}), bf16[16,3,128,128]{3,2,1,0:T(8,128)(2,1)S(1)}, u32[]{:S(2)}, u32[]{:S(2)}) async-start(bf16[16,3,128,128]{3,2,1,0:T(8,128)(2,1)} %copy-done.2), calls=%async_computation.3 | async-start | bytes 3145728 | tf_op jit(solution)/shard_map/all_to_all | solution.py:332
  123.4 4.0 %collective-permute-start.1 = (bf16[7,2,128,128]{3,2,1,0:T(8,128)(2,1)S(1)}, bf16[7,2,128,128]{3,2,1,0:T(8,128)(2,1)S(1)}, u32[]{:S(2)}, u32[]{:S(2)}) collective-permute-start(bf16[7,2,128,128]{3,2,1,0:T(8,128)(2,1)S(1)} %slice.8), channel_id=1, source_target_pairs={{0,16},{1,17},{2,18},{3,19},{4,20},{5,21},{6,22},{7,23},{8,24},{9,... | collective-permute-start | bytes 1376264 | tf_op jit(solution)/shard_map/ppermute | solution.py:244
  127.4 1.6 copy-done.1
  129.0 7.5 %inner.2 = (bf16[16,3,128,128]{3,2,1,0:T(8,128)(2,1)S(1)}, f32[8,2,128,128]{3,2,1,0:T(8,128)S(1)}, f32[8,2,128,128]{3,2,1,0:T(8,128)S(1)}, bf16[7,2,128,128]{3,2,1,0:T(8,128)(2,1)S(1)}) custom-call(s32[17]{0:T(128)S(1)} %pad_add_fusion.st_ref, bf16[16,4,128,128]{3,2,1,0:T(8,128)(2,1)S(1)} %copy-done.1), custom_call_target="tpu_custom_call" | custom-call | flops 8000000000 | bytes 6291456 | tf_op jit(solution)/shard_map/inner/pallas_call | solution.py:254
  136.4 2.2 %collective-permute-start = (bf16[7,2,128,128]{3,2,1,0:T(8,128)(2,1)S(1)}, bf16[7,2,128,128]{3,2,1,0:T(8,128)(2,1)S(1)}, u32[]{:S(2)}, u32[]{:S(2)}) collective-permute-start(bf16[7,2,128,128]{3,2,1,0:T(8,128)(2,1)S(1)} %get-tuple-element.21), channel_id=1, source_target_pairs={{16,0},{17,1},{18,2},{19,3},{20,4},{21,5},{22,6},{23,7},{24,8},{25... | collective-permute-start | bytes 1376264 | tf_op jit(solution)/shard_map/ppermute | solution.py:244
  139.8 4.8 %collective-permute-start.2 = (f32[4,8,256]{2,1,0:T(8,128)S(1)}, f32[4,8,256]{2,1,0:T(8,128)S(1)}, u32[]{:S(2)}, u32[]{:S(2)}) collective-permute-start(f32[4,8,256]{2,1,0:T(8,128)S(1)} %get-tuple-element.24), channel_id=1, source_target_pairs={{16,0},{17,1},{18,2},{19,3},{20,4},{21,5},{22,6},{23,7},{24,8},{25... | collective-permute-start | bytes 98312 | tf_op jit(solution)/shard_map/ppermute | solution.py:244
  144.6 7.9 %collective-permute-done.near_ref = bf16[7,2,128,128]{3,2,1,0:T(8,128)(2,1)S(1)} collective-permute-done((bf16[7,2,128,128]{3,2,1,0:T(8,128)(2,1)S(1)}, bf16[7,2,128,128]{3,2,1,0:T(8,128)(2,1)S(1)}, u32[]{:S(2)}, u32[]{:S(2)}) %collective-permute-start) | collective-permute-done | bytes 458784 | tf_op jit(solution)/shard_map/ppermute | solution.py:244
  153.2 1.6 tail.2
  156.0 4.8 %all-to-all-done.3.back_ref = bf16[16,3,128,128]{3,2,1,0:T(8,128)(2,1)S(1)} async-done(((bf16[16,3,128,128]{3,2,1,0:T(8,128)(2,1)}), bf16[16,3,128,128]{3,2,1,0:T(8,128)(2,1)S(1)}, u32[]{:S(2)}, u32[]{:S(2)}) %all-to-all-start.3) | async-done | bytes 1572896 | tf_op jit(solution)/shard_map/all_to_all | solution.py:332
  160.7 4.3 %all-to-all-start.1 = ((bf16[16,3,128,128]{3,2,1,0:T(8,128)(2,1)}), bf16[16,3,128,128]{3,2,1,0:T(8,128)(2,1)S(1)}, u32[]{:S(2)}, u32[]{:S(2)}) async-start(bf16[16,3,128,128]{3,2,1,0:T(8,128)(2,1)} %copy-done.3), calls=%async_computation.1 | async-start | bytes 3145728 | tf_op jit(solution)/shard_map/all_to_all | solution.py:332
  166.5 36.9 %all-to-all-done.1.back_ref = bf16[16,3,128,128]{3,2,1,0:T(8,128)(2,1)S(1)} async-done(((bf16[16,3,128,128]{3,2,1,0:T(8,128)(2,1)}), bf16[16,3,128,128]{3,2,1,0:T(8,128)(2,1)S(1)}, u32[]{:S(2)}, u32[]{:S(2)}) %all-to-all-start.1) | async-done | bytes 1572896 | tf_op jit(solution)/shard_map/all_to_all | solution.py:332
  (21 shorter events, 13.1 us)
Async XLA Ops:
  3.8 58.2 %all-to-all-start.2 = ((bf16[16,4,128,128]{3,2,1,0:T(8,128)(2,1)}), bf16[16,4,128,128]{3,2,1,0:T(8,128)(2,1)}, u32[]{:S(2)}, u32[]{:S(2)}) async-start(bf16[16,4,128,128]{3,2,1,0:T(8,128)(2,1)} %pack.3), calls=%async_computation.2 | async-start | bytes 4194304 | tf_op jit(solution)/shard_map/all_to_all | solution.py:332
  16.2 50.8 %copy-start.4 = (s32[256]{0:T(256)S(1)}, s32[256]{0:T(256)}, u32[]{:S(2)}) copy-start(s32[256]{0:T(256)} %param.9) | copy-start | bytes 3076
  62.1 53.9 %all-to-all-start = ((bf16[16,4,128,128]{3,2,1,0:T(8,128)(2,1)}), bf16[16,4,128,128]{3,2,1,0:T(8,128)(2,1)S(1)}, u32[]{:S(2)}, u32[]{:S(2)}) async-start(bf16[16,4,128,128]{3,2,1,0:T(8,128)(2,1)} %pack.2), calls=%async_computation | async-start | bytes 4194304 | tf_op jit(solution)/shard_map/all_to_all | solution.py:332
  71.5 15.4 %collective-permute-start.4 = (bf16[7,2,128,128]{3,2,1,0:T(8,128)(2,1)S(1)}, bf16[7,2,128,128]{3,2,1,0:T(8,128)(2,1)S(1)}, u32[]{:S(2)}, u32[]{:S(2)}) collective-permute-start(bf16[7,2,128,128]{3,2,1,0:T(8,128)(2,1)S(1)} %slice.9), channel_id=1, source_target_pairs={{0,16},{1,17},{2,18},{3,19},{4,20},{5,21},{6,22},{7,23},{8,24},{9,... | collective-permute-start | bytes 1376264 | tf_op jit(solution)/shard_map/ppermute | solution.py:244
  83.8 16.0 %collective-permute-start.3 = (bf16[7,2,128,128]{3,2,1,0:T(8,128)(2,1)S(1)}, bf16[7,2,128,128]{3,2,1,0:T(8,128)(2,1)S(1)}, u32[]{:S(2)}, u32[]{:S(2)}) collective-permute-start(bf16[7,2,128,128]{3,2,1,0:T(8,128)(2,1)S(1)} %get-tuple-element.27), channel_id=1, source_target_pairs={{16,0},{17,1},{18,2},{19,3},{20,4},{21,5},{22,6},{23,7},{24,8},{25... | collective-permute-start | bytes 1376264 | tf_op jit(solution)/shard_map/ppermute | solution.py:244
  88.5 11.9 %collective-permute-start.5 = (f32[4,8,256]{2,1,0:T(8,128)S(1)}, f32[4,8,256]{2,1,0:T(8,128)S(1)}, u32[]{:S(2)}, u32[]{:S(2)}) collective-permute-start(f32[4,8,256]{2,1,0:T(8,128)S(1)} %get-tuple-element.30), channel_id=1, source_target_pairs={{16,0},{17,1},{18,2},{19,3},{20,4},{21,5},{22,6},{23,7},{24,8},{25... | collective-permute-start | bytes 98312 | tf_op jit(solution)/shard_map/ppermute | solution.py:244
  102.8 1.1 copy-start.2
  116.0 1.3 copy-start
  117.3 43.4 %all-to-all-start.3 = ((bf16[16,3,128,128]{3,2,1,0:T(8,128)(2,1)}), bf16[16,3,128,128]{3,2,1,0:T(8,128)(2,1)S(1)}, u32[]{:S(2)}, u32[]{:S(2)}) async-start(bf16[16,3,128,128]{3,2,1,0:T(8,128)(2,1)} %copy-done.2), calls=%async_computation.3 | async-start | bytes 3145728 | tf_op jit(solution)/shard_map/all_to_all | solution.py:332
  123.4 15.5 %collective-permute-start.1 = (bf16[7,2,128,128]{3,2,1,0:T(8,128)(2,1)S(1)}, bf16[7,2,128,128]{3,2,1,0:T(8,128)(2,1)S(1)}, u32[]{:S(2)}, u32[]{:S(2)}) collective-permute-start(bf16[7,2,128,128]{3,2,1,0:T(8,128)(2,1)S(1)} %slice.8), channel_id=1, source_target_pairs={{0,16},{1,17},{2,18},{3,19},{4,20},{5,21},{6,22},{7,23},{8,24},{9,... | collective-permute-start | bytes 1376264 | tf_op jit(solution)/shard_map/ppermute | solution.py:244
  127.4 1.6 copy-start.1
  136.4 16.0 %collective-permute-start = (bf16[7,2,128,128]{3,2,1,0:T(8,128)(2,1)S(1)}, bf16[7,2,128,128]{3,2,1,0:T(8,128)(2,1)S(1)}, u32[]{:S(2)}, u32[]{:S(2)}) collective-permute-start(bf16[7,2,128,128]{3,2,1,0:T(8,128)(2,1)S(1)} %get-tuple-element.21), channel_id=1, source_target_pairs={{16,0},{17,1},{18,2},{19,3},{20,4},{21,5},{22,6},{23,7},{24,8},{25... | collective-permute-start | bytes 1376264 | tf_op jit(solution)/shard_map/ppermute | solution.py:244
  139.8 13.4 %collective-permute-start.2 = (f32[4,8,256]{2,1,0:T(8,128)S(1)}, f32[4,8,256]{2,1,0:T(8,128)S(1)}, u32[]{:S(2)}, u32[]{:S(2)}) collective-permute-start(f32[4,8,256]{2,1,0:T(8,128)S(1)} %get-tuple-element.24), channel_id=1, source_target_pairs={{16,0},{17,1},{18,2},{19,3},{20,4},{21,5},{22,6},{23,7},{24,8},{25... | collective-permute-start | bytes 98312 | tf_op jit(solution)/shard_map/ppermute | solution.py:244
  154.8 1.2 copy-start.3
  160.7 42.7 %all-to-all-start.1 = ((bf16[16,3,128,128]{3,2,1,0:T(8,128)(2,1)}), bf16[16,3,128,128]{3,2,1,0:T(8,128)(2,1)S(1)}, u32[]{:S(2)}, u32[]{:S(2)}) async-start(bf16[16,3,128,128]{3,2,1,0:T(8,128)(2,1)} %copy-done.3), calls=%async_computation.1 | async-start | bytes 3145728 | tf_op jit(solution)/shard_map/all_to_all | solution.py:332

commit v4 on v3

--- a/solution.py
+++ b/solution.py
@@ -157,24 +157,30 @@
     scale = 1.0 / math.sqrt(width)
     gk_ref[...] = tail_ref[:, GKEY]
     gv_ref[...] = tail_ref[:, GVALUE]
-    rows = REACH * BLOCK
-    q = near_ref[:, 0].reshape(rows, width)
-    d = near_ref[:, 1].reshape(rows, width)
-    lse = jnp.concatenate([stat_ref[t, 0:1, :] for t in range(EDGE // 2)], 1)[:, :rows]
-    delta = jnp.concatenate([stat_ref[t, 1:2, :] for t in range(EDGE // 2)], 1)[:, :rows]
-    live = lse < -MASKED
-    delta = jnp.where(live, delta, 0.0)
-
-    def key_block(j, _):
-        s = across(x_ref[j, KEY], q)
-        dp = across(x_ref[j, VALUE], d)
-        prob = jnp.exp2(s * (scale * LOG2E) - lse)
-        ds = (prob * (dp - delta) * scale).astype(BF16)
-        gv_ref[j] += plain(prob.astype(BF16), d)
-        gk_ref[j] += plain(ds, q)
-        return 0
-
-    lax.fori_loop(st_ref[st_ref.shape[0] - 1], EDGE, key_block, 0)
+    tiles = st_ref[st_ref.shape[0] - 2]
+    for t in range(1, EDGE // 2 + 1):
+
+        @pl.when(tiles == t)
+        def _():
+            many = min(2 * t, REACH)
+            rows = many * BLOCK
+            q = near_ref[:many, 0].reshape(rows, width)
+            d = near_ref[:many, 1].reshape(rows, width)
+            lse = jnp.concatenate([stat_ref[i, 0:1, :] for i in range(t)], 1)[:, :rows]
+            delta = jnp.concatenate([stat_ref[i, 1:2, :] for i in range(t)], 1)[:, :rows]
+            delta = jnp.where(lse < -MASKED, delta, 0.0)
+
+            def key_block(j, _):
+                s = across(x_ref[j, KEY], q)
+                dp = across(x_ref[j, VALUE], d)
+                prob = jnp.exp2(s * (scale * LOG2E) - lse)
+                ds = (prob * (dp - delta) * scale).astype(BF16)
+                gv_ref[j] += plain(prob.astype(BF16), d)
+                gk_ref[j] += plain(ds, q)
+                return 0
+
+            lax.fori_loop(st_ref[st_ref.shape[0] - 1], EDGE, key_block, 0)
+
     out_ref[:, GKEY] = gk_ref[...].astype(BF16)
     out_ref[:, GVALUE] = gv_ref[...].astype(BF16)
 
@@ -200,8 +206,9 @@
 
 SMEM = pl.BlockSpec(memory_space=pltpu.SMEM)
 PARAMS = pltpu.CompilerParams(vmem_limit_bytes=40 * 1024 * 1024)
+WIDE_PARAMS = pltpu.CompilerParams(vmem_limit_bytes=62 * 1024 * 1024)
 PACK_PARAMS = pltpu.CompilerParams(vmem_limit_bytes=60 * 1024 * 1024)
-STEP = 16
+STEP = 8
 
 
 def packed(arrays, half, heads):
@@ -244,7 +251,7 @@
     return lax.ppermute(array, ("blk", "uly"), pairs)
 
 
-def head_grads(starts, x, heads):
+def head_grads(starts, x, heads, params):
     blocks = x.shape[0]
     tile_shape = x.shape[2:]
     far = passed_along(x[blocks - REACH :, KEY : VALUE + 1], heads)
@@ -257,7 +264,7 @@
         in_specs=[SMEM, whole()],
         out_specs=(whole(),) * 4,
         scratch_shapes=[pltpu.VMEM((blocks,) + tile_shape, F32)] * 2,
-        compiler_params=PARAMS,
+        compiler_params=params,
         cost_estimate=pl.CostEstimate(flops=8 * 10**9, bytes_accessed=6 << 20, transcendentals=1 << 20),
         name="inner",
     )(starts, x)
@@ -284,7 +291,7 @@
         scratch_shapes=[pltpu.VMEM((REACH + EDGE,) + tile_shape, BF16)] * 2
         + [pltpu.VMEM((REACH + EDGE,) + tile_shape, F32)] * 2,
         input_output_aliases={4: 0},
-        compiler_params=PARAMS,
+        compiler_params=params,
         cost_estimate=pl.CostEstimate(flops=2 * 10**9, bytes_accessed=3 << 20, transcendentals=1 << 18),
         name="head",
     )(starts, x, far, head_acc, out)
@@ -306,7 +313,7 @@
         out_specs=edge_in(2, at_end),
         scratch_shapes=[pltpu.VMEM((EDGE,) + tile_shape, F32)] * 2,
         input_output_aliases={5: 0},
-        compiler_params=PARAMS,
+        compiler_params=params,
         cost_estimate=pl.CostEstimate(flops=2 * 10**9, bytes_accessed=3 << 20, transcendentals=1 << 18),
         name="tail",
     )(starts, x, near, stats, tail_acc, out)
@@ -324,9 +331,11 @@
     segment = lax.axis_index("blk") * PHASES + lax.axis_index("uly") // heads
     last = lax.axis_size("blk") * PHASES - 1
     own = lax.dynamic_slice_in_dim(doc_start, segment * blocks, blocks, 0) // BLOCK - segment * blocks
-    after = lax.dynamic_slice_in_dim(doc_start, jnp.minimum(segment + 1, last) * blocks, 1, 0) // BLOCK
-    after = jnp.where(segment == last, EDGE, after - segment * blocks - (blocks - EDGE))
-    starts = jnp.concatenate([own, after]).astype(jnp.int32)
+    following = jnp.minimum(segment + 1, last) * blocks
+    heads_of = lax.dynamic_slice_in_dim(doc_start, following, EDGE, 0) // BLOCK
+    tiles = (jnp.sum(heads_of < following) + 1) // 2
+    after = jnp.where(segment == last, EDGE, heads_of[0] - segment * blocks - (blocks - EDGE))
+    starts = jnp.concatenate([own, jnp.stack([tiles, after])]).astype(jnp.int32)
 
     def exchanged(array):
         return lax.all_to_all(
@@ -335,7 +344,7 @@
 
     arrays = (queries, grad_out, keys, values)
     inputs = [exchanged(packed(arrays, p, heads)) for p in range(PHASES)]
-    grads = [exchanged(head_grads(starts, x, heads)) for x in inputs]
+    grads = [exchanged(head_grads(starts, x, heads, p)) for x, p in zip(inputs, (WIDE_PARAMS, PARAMS))]
     outs = ()
     for p in range(PHASES):
         outs = unpacked(grads[p], p, outs)

time: 207 us -> 205 us (level)
  Pallas kernels: 32.1 us -> 44.4 us
  waiting for transfers between devices: 117 us -> 110 us
  local copies, waits for them, and re-layouts: 7.9 us -> 3.68 us
  starting transfers between devices: 44.9 us -> 41.5 us
    pallas_call x2, Pallas kernels: 2.64 us -> 10.4 us  [head_grads(): pl.pallas_call(head_kernel, grid=(1,), out_shape=(out_type, jax.ShapeDtyp...]
    pallas_call x2, Pallas kernels: 3.91 us -> 8.71 us  [head_grads(): pl.pallas_call(tail_kernel, grid=(1,), out_shape=out_type, in_specs=[SMEM...]
    ppermute x6, waiting for transfers between devices: 16.9 us -> 12.3 us  [passed_along(): return lax.ppermute(array, ('blk', 'uly'), pairs)]
    ppermute x6, starting transfers between devices: 21.5 us -> 18.1 us  [passed_along(): return lax.ppermute(array, ('blk', 'uly'), pairs)]
    unnamed x10 -> x14, local copies, waits for them, and re-layouts: 5.21 us -> 2.6 us
  transfers between devices with their start and end apart: 10 -> 10, of which waited for: 10 -> 9; matrix products, arithmetic and copies ran while one was open for 1% -> 1% of each run, Pallas kernels for 13% -> 20%
where the time goes in v4:
time: 205 us; the launch traced here: 203 us
  waiting for transfers between devices  110 us (54%)
  Pallas kernels  44.4 us (22%)
  starting transfers between devices  41.5 us (20%)
  local copies, waits for them, and re-layouts  3.68 us (2%)
    all_to_all x4, waiting for transfers between devices, exchanged(): lax.all_to_all(array, 'uly', split_axis=0, concat_axis=0, tiled=True, axi...  98.2 us
    all_to_all x4, starting transfers between devices, exchanged(): lax.all_to_all(array, 'uly', split_axis=0, concat_axis=0, tiled=True, axi...  23.4 us
    ppermute x6, starting transfers between devices, passed_along(): return lax.ppermute(array, ('blk', 'uly'), pairs)  18.1 us
    pallas_call x2, Pallas kernels, head_grads(): pl.pallas_call(inner_kernel, out_shape=(out_type, edge_type, edge_type, n...  17.2 us
    ppermute x6, waiting for transfers between devices, passed_along(): return lax.ppermute(array, ('blk', 'uly'), pairs)  12.3 us
    pallas_call x2, Pallas kernels, head_grads(): pl.pallas_call(head_kernel, grid=(1,), out_shape=(out_type, jax.ShapeDtyp...  10.4 us
    pallas_call x2, Pallas kernels, head_grads(): pl.pallas_call(tail_kernel, grid=(1,), out_shape=out_type, in_specs=[SMEM...  8.71 us
    pallas_call x2, Pallas kernels, packed(): pl.pallas_call(pack_kernel, grid=(steps,), out_shape=jax.ShapeDtypeStruct...  5.42 us
  transfers between devices with their start and end apart: 10, of which 9 were waited for; matrix products, arithmetic and copies ran while one was open for 1% of the time, Pallas kernels for 20%

profile of v4, /device:TPU:23, one launch (start us, length us, event | category | flops | bytes accessed | tf_op | source)
XLA Modules:
  0.0 202.9 jit_solution(16338716385680627045)
XLA Ops:
  0.6 2.7 %pack.3 = bf16[16,4,128,128]{3,2,1,0:T(8,128)(2,1)} custom-call(bf16[128,4096]{1,0:T(8,128)(2,1)} %refs_0_.3, bf16[128,4096]{1,0:T(8,128)(2,1)} %refs_1_.3, bf16[128,4096]{1,0:T(8,128)(2,1)} %refs_2_.3, bf16[128,4096]{1,0:T(8,128)(2,1)} %refs_3_.3), custom_call_target="tpu_custom_call" | custom-call | bytes 4194304 | tf_op jit(solution)/shard_map/pack/pallas_call | solution.py:218
  3.3 9.2 %all-to-all-start.2 = ((bf16[16,4,128,128]{3,2,1,0:T(8,128)(2,1)}), bf16[16,4,128,128]{3,2,1,0:T(8,128)(2,1)S(1)}, u32[]{:S(2)}, u32[]{:S(2)}) async-start(bf16[16,4,128,128]{3,2,1,0:T(8,128)(2,1)} %pack.3), calls=%async_computation.2 | async-start | bytes 4194304 | tf_op jit(solution)/shard_map/all_to_all | solution.py:341
  12.5 2.7 %pack.2 = bf16[16,4,128,128]{3,2,1,0:T(8,128)(2,1)} custom-call(bf16[128,4096]{1,0:T(8,128)(2,1)} %refs_0_.3, bf16[128,4096]{1,0:T(8,128)(2,1)} %refs_1_.3, bf16[128,4096]{1,0:T(8,128)(2,1)} %refs_2_.3, bf16[128,4096]{1,0:T(8,128)(2,1)} %refs_3_.3), custom_call_target="tpu_custom_call" | custom-call | bytes 4194304 | tf_op jit(solution)/shard_map/pack/pallas_call | solution.py:218
  15.2 46.2 %all-to-all-done.2.x_ref = bf16[16,4,128,128]{3,2,1,0:T(8,128)(2,1)S(1)} async-done(((bf16[16,4,128,128]{3,2,1,0:T(8,128)(2,1)}), bf16[16,4,128,128]{3,2,1,0:T(8,128)(2,1)S(1)}, u32[]{:S(2)}, u32[]{:S(2)}) %all-to-all-start.2) | async-done | bytes 2097184 | tf_op jit(solution)/shard_map/all_to_all | solution.py:341
  61.4 5.0 %all-to-all-start = ((bf16[16,4,128,128]{3,2,1,0:T(8,128)(2,1)}), bf16[16,4,128,128]{3,2,1,0:T(8,128)(2,1)}, u32[]{:S(2)}, u32[]{:S(2)}) async-start(bf16[16,4,128,128]{3,2,1,0:T(8,128)(2,1)} %pack.2), calls=%async_computation | async-start | bytes 4194304 | tf_op jit(solution)/shard_map/all_to_all | solution.py:341
  68.6 3.8 %collective-permute-start.4 = (bf16[7,2,128,128]{3,2,1,0:T(8,128)(2,1)S(1)}, bf16[7,2,128,128]{3,2,1,0:T(8,128)(2,1)S(1)}, u32[]{:S(2)}, u32[]{:S(2)}) collective-permute-start(bf16[7,2,128,128]{3,2,1,0:T(8,128)(2,1)S(1)} %slice.13), channel_id=1, source_target_pairs={{0,16},{1,17},{2,18},{3,19},{4,20},{5,21},{6,22},{7,23},{8,24},{9,... | collective-permute-start | bytes 1376264 | tf_op jit(solution)/shard_map/ppermute | solution.py:251
  72.3 9.5 %inner.3 = (bf16[16,3,128,128]{3,2,1,0:T(8,128)(2,1)}, f32[8,2,128,128]{3,2,1,0:T(8,128)}, f32[8,2,128,128]{3,2,1,0:T(8,128)}, bf16[7,2,128,128]{3,2,1,0:T(8,128)(2,1)}) custom-call(s32[18]{0:T(128)} %pad_add_fusion.st_ref, bf16[16,4,128,128]{3,2,1,0:T(8,128)(2,1)} %copy-done.2), custom_call_target="tpu_custom_call" | custom-call | flops 8000000000 | bytes 6291456 | tf_op jit(solution)/shard_map/inner/pallas_call | solution.py:261
  81.9 3.1 %collective-permute-start.3 = (bf16[7,2,128,128]{3,2,1,0:T(8,128)(2,1)}, bf16[7,2,128,128]{3,2,1,0:T(8,128)(2,1)S(1)}, u32[]{:S(2)}, u32[]{:S(2)}) collective-permute-start(bf16[7,2,128,128]{3,2,1,0:T(8,128)(2,1)} %get-tuple-element.27), channel_id=1, source_target_pairs={{16,0},{17,1},{18,2},{19,3},{20,4},{21,5},{22,6},{23,7},{24,8},{25... | collective-permute-start | bytes 1376264 | tf_op jit(solution)/shard_map/ppermute | solution.py:251
  85.8 6.0 %head.3 = (bf16[16,3,128,128]{3,2,1,0:T(8,128)(2,1)}, f32[4,8,256]{2,1,0:T(8,128)}) custom-call(s32[18]{0:T(128)} %pad_add_fusion.st_ref, bf16[16,4,128,128]{3,2,1,0:T(8,128)(2,1)} %copy-done.2, bf16[7,2,128,128]{3,2,1,0:T(8,128)(2,1)} %copy-done.5, f32[8,2,128,128]{3,2,1,0:T(8,128)} %get-tuple-element.28.head_ref, ...), custom_call_target="tpu_custom_call", output_to_operand_aliasing={{0}: (4, {})} | custom-call | flops 2000000000 | bytes 3145728 | tf_op jit(solution)/shard_map/head/pallas_call | solution.py:279
  91.8 1.9 collective-permute-start.5
  93.7 4.3 %collective-permute-done.3.near_ref = bf16[7,2,128,128]{3,2,1,0:T(8,128)(2,1)S(1)} collective-permute-done((bf16[7,2,128,128]{3,2,1,0:T(8,128)(2,1)}, bf16[7,2,128,128]{3,2,1,0:T(8,128)(2,1)S(1)}, u32[]{:S(2)}, u32[]{:S(2)}) %collective-permute-start.3) | collective-permute-done | bytes 458784 | tf_op jit(solution)/shard_map/ppermute | solution.py:251
  99.6 5.0 %tail.3 = bf16[16,3,128,128]{3,2,1,0:T(8,128)(2,1)} custom-call(s32[18]{0:T(128)} %pad_add_fusion.st_ref, bf16[16,4,128,128]{3,2,1,0:T(8,128)(2,1)} %copy-done.2, bf16[7,2,128,128]{3,2,1,0:T(8,128)(2,1)} %copy-done.4, f32[4,8,256]{2,1,0:T(8,128)} %copy-done.6, f32[8,2,128,128]{3,2,1,0:T(8,128)} %get-tuple-element.31.tail_ref, ...), custom_call_target="tpu_custom_call", output_to_operand_aliasing={{}: (5, {})} | custom-call | flops 2000000000 | bytes 3145728 | tf_op jit(solution)/shard_map/tail/pallas_call | solution.py:301
  104.6 10.9 %all-to-all-done.x_ref = bf16[16,4,128,128]{3,2,1,0:T(8,128)(2,1)} async-done(((bf16[16,4,128,128]{3,2,1,0:T(8,128)(2,1)}), bf16[16,4,128,128]{3,2,1,0:T(8,128)(2,1)}, u32[]{:S(2)}, u32[]{:S(2)}) %all-to-all-start) | async-done | bytes 2097184 | tf_op jit(solution)/shard_map/all_to_all | solution.py:341
  115.5 5.0 %all-to-all-start.3 = ((bf16[16,3,128,128]{3,2,1,0:T(8,128)(2,1)}), bf16[16,3,128,128]{3,2,1,0:T(8,128)(2,1)S(1)}, u32[]{:S(2)}, u32[]{:S(2)}) async-start(bf16[16,3,128,128]{3,2,1,0:T(8,128)(2,1)} %tail.3), calls=%async_computation.3 | async-start | bytes 3145728 | tf_op jit(solution)/shard_map/all_to_all | solution.py:341
  121.5 4.0 %collective-permute-start.1 = (bf16[7,2,128,128]{3,2,1,0:T(8,128)(2,1)S(1)}, bf16[7,2,128,128]{3,2,1,0:T(8,128)(2,1)S(1)}, u32[]{:S(2)}, u32[]{:S(2)}) collective-permute-start(bf16[7,2,128,128]{3,2,1,0:T(8,128)(2,1)S(1)} %slice.12), channel_id=1, source_target_pairs={{0,16},{1,17},{2,18},{3,19},{4,20},{5,21},{6,22},{7,23},{8,24},{9,... | collective-permute-start | bytes 1376264 | tf_op jit(solution)/shard_map/ppermute | solution.py:251
  125.5 7.7 %inner.2 = (bf16[16,3,128,128]{3,2,1,0:T(8,128)(2,1)S(1)}, f32[8,2,128,128]{3,2,1,0:T(8,128)S(1)}, f32[8,2,128,128]{3,2,1,0:T(8,128)S(1)}, bf16[7,2,128,128]{3,2,1,0:T(8,128)(2,1)S(1)}) custom-call(s32[18]{0:T(128)S(1)} %copy-done.1, bf16[16,4,128,128]{3,2,1,0:T(8,128)(2,1)} %all-to-all-done.x_ref), custom_call_target="tpu_custom_call" | custom-call | flops 8000000000 | bytes 6291456 | tf_op jit(solution)/shard_map/inner/pallas_call | solution.py:261
  133.2 3.2 %collective-permute-start = (bf16[7,2,128,128]{3,2,1,0:T(8,128)(2,1)S(1)}, bf16[7,2,128,128]{3,2,1,0:T(8,128)(2,1)S(1)}, u32[]{:S(2)}, u32[]{:S(2)}) collective-permute-start(bf16[7,2,128,128]{3,2,1,0:T(8,128)(2,1)S(1)} %get-tuple-element.21), channel_id=1, source_target_pairs={{16,0},{17,1},{18,2},{19,3},{20,4},{21,5},{22,6},{23,7},{24,8},{25... | collective-permute-start | bytes 1376264 | tf_op jit(solution)/shard_map/ppermute | solution.py:251
  137.0 4.4 %head.2 = (bf16[16,3,128,128]{3,2,1,0:T(8,128)(2,1)S(1)}, f32[4,8,256]{2,1,0:T(8,128)S(1)}) custom-call(s32[18]{0:T(128)S(1)} %copy-done.1, bf16[16,4,128,128]{3,2,1,0:T(8,128)(2,1)} %all-to-all-done.x_ref, bf16[7,2,128,128]{3,2,1,0:T(8,128)(2,1)S(1)} %collective-permute-done.1.far_ref, ...), custom_call_target="tpu_custom_call", output_to_operand_aliasing={{0}: (4, {})} | custom-call | flops 2000000000 | bytes 3145728 | tf_op jit(solution)/shard_map/head/pallas_call | solution.py:279
  141.4 2.2 %collective-permute-start.2 = (f32[4,8,256]{2,1,0:T(8,128)S(1)}, f32[4,8,256]{2,1,0:T(8,128)S(1)}, u32[]{:S(2)}, u32[]{:S(2)}) collective-permute-start(f32[4,8,256]{2,1,0:T(8,128)S(1)} %get-tuple-element.24), channel_id=1, source_target_pairs={{16,0},{17,1},{18,2},{19,3},{20,4},{21,5},{22,6},{23,7},{24,8},{25... | collective-permute-start | bytes 98312 | tf_op jit(solution)/shard_map/ppermute | solution.py:251
  143.6 5.6 %collective-permute-done.near_ref = bf16[7,2,128,128]{3,2,1,0:T(8,128)(2,1)S(1)} collective-permute-done((bf16[7,2,128,128]{3,2,1,0:T(8,128)(2,1)S(1)}, bf16[7,2,128,128]{3,2,1,0:T(8,128)(2,1)S(1)}, u32[]{:S(2)}, u32[]{:S(2)}) %collective-permute-start) | collective-permute-done | bytes 458784 | tf_op jit(solution)/shard_map/ppermute | solution.py:251
  149.9 3.7 %tail.2 = bf16[16,3,128,128]{3,2,1,0:T(8,128)(2,1)S(1)} custom-call(s32[18]{0:T(128)S(1)} %copy-done.1, bf16[16,4,128,128]{3,2,1,0:T(8,128)(2,1)} %all-to-all-done.x_ref, bf16[7,2,128,128]{3,2,1,0:T(8,128)(2,1)S(1)} %collective-permute-done.near_ref, f32[4,8,256]{2,1,0:T(8,128)S(1)} %collective-permute-done.2.stat_ref, ...), custom_call_target="tpu_custom_call", output_to_operand_aliasing={{}: (5, {})} | custom-call | flops 2000000000 | bytes 3145728 | tf_op jit(solution)/shard_map/tail/pallas_call | solution.py:301
  154.9 4.0 %all-to-all-done.3.back_ref = bf16[16,3,128,128]{3,2,1,0:T(8,128)(2,1)S(1)} async-done(((bf16[16,3,128,128]{3,2,1,0:T(8,128)(2,1)}), bf16[16,3,128,128]{3,2,1,0:T(8,128)(2,1)S(1)}, u32[]{:S(2)}, u32[]{:S(2)}) %all-to-all-start.3) | async-done | bytes 1572896 | tf_op jit(solution)/shard_map/all_to_all | solution.py:341
  158.9 4.3 %all-to-all-start.1 = ((bf16[16,3,128,128]{3,2,1,0:T(8,128)(2,1)}), bf16[16,3,128,128]{3,2,1,0:T(8,128)(2,1)S(1)}, u32[]{:S(2)}, u32[]{:S(2)}) async-start(bf16[16,3,128,128]{3,2,1,0:T(8,128)(2,1)} %copy-done), calls=%async_computation.1 | async-start | bytes 3145728 | tf_op jit(solution)/shard_map/all_to_all | solution.py:341
  164.5 37.1 %all-to-all-done.1.back_ref = bf16[16,3,128,128]{3,2,1,0:T(8,128)(2,1)S(1)} async-done(((bf16[16,3,128,128]{3,2,1,0:T(8,128)(2,1)}), bf16[16,3,128,128]{3,2,1,0:T(8,128)(2,1)S(1)}, u32[]{:S(2)}, u32[]{:S(2)}) %all-to-all-start.1) | async-done | bytes 1572896 | tf_op jit(solution)/shard_map/all_to_all | solution.py:341
  (25 shorter events, 10.1 us)
Async XLA Ops:
  3.3 58.1 %all-to-all-start.2 = ((bf16[16,4,128,128]{3,2,1,0:T(8,128)(2,1)}), bf16[16,4,128,128]{3,2,1,0:T(8,128)(2,1)S(1)}, u32[]{:S(2)}, u32[]{:S(2)}) async-start(bf16[16,4,128,128]{3,2,1,0:T(8,128)(2,1)} %pack.3), calls=%async_computation.2 | async-start | bytes 4194304 | tf_op jit(solution)/shard_map/all_to_all | solution.py:341
  15.2 51.2 %copy-start.3 = (s32[256]{0:T(256)S(1)}, s32[256]{0:T(256)}, u32[]{:S(2)}) copy-start(s32[256]{0:T(256)} %param.9) | copy-start | bytes 3076
  61.4 7.1 %copy-start.2 = (bf16[16,4,128,128]{3,2,1,0:T(8,128)(2,1)}, bf16[16,4,128,128]{3,2,1,0:T(8,128)(2,1)S(1)}, u32[]{:S(2)}) copy-start(bf16[16,4,128,128]{3,2,1,0:T(8,128)(2,1)S(1)} %all-to-all-done.2.x_ref) | copy-start | bytes 6291460
  61.4 54.0 %all-to-all-start = ((bf16[16,4,128,128]{3,2,1,0:T(8,128)(2,1)}), bf16[16,4,128,128]{3,2,1,0:T(8,128)(2,1)}, u32[]{:S(2)}, u32[]{:S(2)}) async-start(bf16[16,4,128,128]{3,2,1,0:T(8,128)(2,1)} %pack.2), calls=%async_computation | async-start | bytes 4194304 | tf_op jit(solution)/shard_map/all_to_all | solution.py:341
  68.6 16.4 %collective-permute-start.4 = (bf16[7,2,128,128]{3,2,1,0:T(8,128)(2,1)S(1)}, bf16[7,2,128,128]{3,2,1,0:T(8,128)(2,1)S(1)}, u32[]{:S(2)}, u32[]{:S(2)}) collective-permute-start(bf16[7,2,128,128]{3,2,1,0:T(8,128)(2,1)S(1)} %slice.13), channel_id=1, source_target_pairs={{0,16},{1,17},{2,18},{3,19},{4,20},{5,21},{6,22},{7,23},{8,24},{9,... | collective-permute-start | bytes 1376264 | tf_op jit(solution)/shard_map/ppermute | solution.py:251
  81.9 16.1 %collective-permute-start.3 = (bf16[7,2,128,128]{3,2,1,0:T(8,128)(2,1)}, bf16[7,2,128,128]{3,2,1,0:T(8,128)(2,1)S(1)}, u32[]{:S(2)}, u32[]{:S(2)}) collective-permute-start(bf16[7,2,128,128]{3,2,1,0:T(8,128)(2,1)} %get-tuple-element.27), channel_id=1, source_target_pairs={{16,0},{17,1},{18,2},{19,3},{20,4},{21,5},{22,6},{23,7},{24,8},{25... | collective-permute-start | bytes 1376264 | tf_op jit(solution)/shard_map/ppermute | solution.py:251
  85.0 0.8 copy-start.5
  91.8 7.3 %collective-permute-start.5 = (f32[4,8,256]{2,1,0:T(8,128)}, f32[4,8,256]{2,1,0:T(8,128)S(1)}, u32[]{:S(2)}, u32[]{:S(2)}) collective-permute-start(f32[4,8,256]{2,1,0:T(8,128)} %get-tuple-element.30), channel_id=1, source_target_pairs={{16,0},{17,1},{18,2},{19,3},{20,4},{21,5},{22,6},{23,7},{24,8},{25... | collective-permute-start | bytes 98312 | tf_op jit(solution)/shard_map/ppermute | solution.py:251
  98.0 1.0 copy-start.4
  99.0 0.6 copy-start.6
  104.6 20.9 %copy-start.1 = (s32[18]{0:T(128)S(1)}, s32[18]{0:T(128)}, u32[]{:S(2)}) copy-start(s32[18]{0:T(128)} %pad_add_fusion.st_ref) | copy-start | bytes 220
  115.5 43.4 %all-to-all-start.3 = ((bf16[16,3,128,128]{3,2,1,0:T(8,128)(2,1)}), bf16[16,3,128,128]{3,2,1,0:T(8,128)(2,1)S(1)}, u32[]{:S(2)}, u32[]{:S(2)}) async-start(bf16[16,3,128,128]{3,2,1,0:T(8,128)(2,1)} %tail.3), calls=%async_computation.3 | async-start | bytes 3145728 | tf_op jit(solution)/shard_map/all_to_all | solution.py:341
  121.5 15.5 %collective-permute-start.1 = (bf16[7,2,128,128]{3,2,1,0:T(8,128)(2,1)S(1)}, bf16[7,2,128,128]{3,2,1,0:T(8,128)(2,1)S(1)}, u32[]{:S(2)}, u32[]{:S(2)}) collective-permute-start(bf16[7,2,128,128]{3,2,1,0:T(8,128)(2,1)S(1)} %slice.12), channel_id=1, source_target_pairs={{0,16},{1,17},{2,18},{3,19},{4,20},{5,21},{6,22},{7,23},{8,24},{9,... | collective-permute-start | bytes 1376264 | tf_op jit(solution)/shard_map/ppermute | solution.py:251
  133.2 16.1 %collective-permute-start = (bf16[7,2,128,128]{3,2,1,0:T(8,128)(2,1)S(1)}, bf16[7,2,128,128]{3,2,1,0:T(8,128)(2,1)S(1)}, u32[]{:S(2)}, u32[]{:S(2)}) collective-permute-start(bf16[7,2,128,128]{3,2,1,0:T(8,128)(2,1)S(1)} %get-tuple-element.21), channel_id=1, source_target_pairs={{16,0},{17,1},{18,2},{19,3},{20,4},{21,5},{22,6},{23,7},{24,8},{25... | collective-permute-start | bytes 1376264 | tf_op jit(solution)/shard_map/ppermute | solution.py:251
  141.4 8.5 %collective-permute-start.2 = (f32[4,8,256]{2,1,0:T(8,128)S(1)}, f32[4,8,256]{2,1,0:T(8,128)S(1)}, u32[]{:S(2)}, u32[]{:S(2)}) collective-permute-start(f32[4,8,256]{2,1,0:T(8,128)S(1)} %get-tuple-element.24), channel_id=1, source_target_pairs={{16,0},{17,1},{18,2},{19,3},{20,4},{21,5},{22,6},{23,7},{24,8},{25... | collective-permute-start | bytes 98312 | tf_op jit(solution)/shard_map/ppermute | solution.py:251
  153.7 1.2 copy-start
  158.9 42.7 %all-to-all-start.1 = ((bf16[16,3,128,128]{3,2,1,0:T(8,128)(2,1)}), bf16[16,3,128,128]{3,2,1,0:T(8,128)(2,1)S(1)}, u32[]{:S(2)}, u32[]{:S(2)}) async-start(bf16[16,3,128,128]{3,2,1,0:T(8,128)(2,1)} %copy-done), calls=%async_computation.1 | async-start | bytes 3145728 | tf_op jit(solution)/shard_map/all_to_all | solution.py:341

commit v5 on v4

--- a/solution.py
+++ b/solution.py
@@ -90,14 +90,14 @@
 
         return 0
 
-    lax.fori_loop(0, blocks // 2, tile, 0)
+    lax.fori_loop(EDGE // 2, blocks // 2, tile, 0)
 
     def store(i, _):
         out_ref[i, GKEY] = gk_ref[i].astype(BF16)
         out_ref[i, GVALUE] = gv_ref[i].astype(BF16)
         return 0
 
-    lax.fori_loop(0, blocks, store, 0)
+    lax.fori_loop(EDGE, blocks, store, 0)
     head_ref[:, GKEY] = gk_ref[:EDGE]
     head_ref[:, GVALUE] = gv_ref[:EDGE]
     tail_ref[:, GKEY] = gk_ref[blocks - EDGE :]
@@ -107,6 +107,7 @@
 def head_kernel(
     st_ref, x_ref, far_ref, head_ref, out_in_ref, out_ref, stat_ref, k_ref, v_ref, gk_ref, gv_ref
 ):
+    del out_in_ref
     width = x_ref.shape[-1]
     k_ref[:REACH] = far_ref[:, 0]
     v_ref[:REACH] = far_ref[:, 1]
@@ -114,16 +115,15 @@
     v_ref[REACH:] = x_ref[:, VALUE]
     gk_ref[REACH:] = head_ref[:, GKEY]
     gv_ref[REACH:] = head_ref[:, GVALUE]
-    out_ref[:, GQUERY] = out_in_ref[:, GQUERY]
     stat_ref[...] = jnp.full(stat_ref.shape, -MASKED, F32)
 
     def tile(t, _):
         first = st_ref[2 * t]
         n_dyn = 2 * t + 2 - first
         second = st_ref[2 * t + 1] - first
-        for n in range(3, MAXB + 2):
-
-            @pl.when((first < 0) & (n_dyn == n))
+        for n in range(2, MAXB + 2):
+
+            @pl.when(n_dyn == n)
             def _():
                 window = pl.ds(first + REACH, n)
                 pair = pl.ds(2 * t, 2)
@@ -140,7 +140,8 @@
                 gv_ref[window] += gv.reshape(n, BLOCK, width)
                 out_ref[pair, GQUERY] = gq.astype(BF16).reshape(2, BLOCK, width)
                 c = lax.broadcasted_iota(jnp.int32, lse.shape, 1)
-                lse = jnp.where((c < BLOCK) | (second == 0), lse, -MASKED)
+                live = (first < 0) & ((c < BLOCK) | (second == 0))
+                lse = jnp.where(live, lse, -MASKED)
                 stat_ref[t, 0:1, :] = lse
                 stat_ref[t, 1:2, :] = delta
 
@@ -265,7 +266,7 @@
         out_specs=(whole(),) * 4,
         scratch_shapes=[pltpu.VMEM((blocks,) + tile_shape, F32)] * 2,
         compiler_params=params,
-        cost_estimate=pl.CostEstimate(flops=8 * 10**9, bytes_accessed=6 << 20, transcendentals=1 << 20),
+        cost_estimate=pl.CostEstimate(flops=5 * 10**9, bytes_accessed=6 << 20, transcendentals=1 << 20),
         name="inner",
     )(starts, x)
 
@@ -285,14 +286,14 @@
             edge_in(4, 0),
             full((REACH, 2) + tile_shape),
             full((EDGE, 2) + tile_shape),
-            edge_in(3, 0),
+            pl.BlockSpec(memory_space=pl.ANY),
         ],
         out_specs=(edge_in(3, 0), full(stat_shape)),
         scratch_shapes=[pltpu.VMEM((REACH + EDGE,) + tile_shape, BF16)] * 2
         + [pltpu.VMEM((REACH + EDGE,) + tile_shape, F32)] * 2,
         input_output_aliases={4: 0},
         compiler_params=params,
-        cost_estimate=pl.CostEstimate(flops=2 * 10**9, bytes_accessed=3 << 20, transcendentals=1 << 18),
+        cost_estimate=pl.CostEstimate(flops=5 * 10**9, bytes_accessed=3 << 20, transcendentals=1 << 18),
         name="head",
     )(starts, x, far, head_acc, out)
     stats = passed_along(stats, -heads)

time: 205 us -> 205 us (level)
  starting transfers between devices: 41.5 us -> 45.4 us
  Pallas kernels: 44.4 us -> 41.1 us
    ppermute x6, starting transfers between devices: 18.1 us -> 22 us  [passed_along(): return lax.ppermute(array, ('blk', 'uly'), pairs)]
    pallas_call x2, Pallas kernels: 17.2 us -> 13.7 us  [head_grads(): pl.pallas_call(inner_kernel, out_shape=(out_type, edge_type, edge_type, n...]
    ppermute x6, waiting for transfers between devices: 12.3 us -> 9.71 us  [passed_along(): return lax.ppermute(array, ('blk', 'uly'), pairs)]
  transfers between devices with their start and end apart: 10 -> 10, of which waited for: 9 -> 10; matrix products, arithmetic and copies ran while one was open for 1% -> 1% of each run, Pallas kernels for 20% -> 18%
where the time goes in v5:
time: 205 us; the launch traced here: 203 us
  waiting for transfers between devices  110 us (54%)
  starting transfers between devices  45.4 us (22%)
  Pallas kernels  41.1 us (20%)
  local copies, waits for them, and re-layouts  3.68 us (2%)
    all_to_all x4, waiting for transfers between devices, exchanged(): lax.all_to_all(array, 'uly', split_axis=0, concat_axis=0, tiled=True, axi...  100 us
    all_to_all x4, starting transfers between devices, exchanged(): lax.all_to_all(array, 'uly', split_axis=0, concat_axis=0, tiled=True, axi...  23.4 us
    ppermute x6, starting transfers between devices, passed_along(): return lax.ppermute(array, ('blk', 'uly'), pairs)  22 us
    pallas_call x2, Pallas kernels, head_grads(): pl.pallas_call(inner_kernel, out_shape=(out_type, edge_type, edge_type, n...  13.7 us
    pallas_call x2, Pallas kernels, head_grads(): pl.pallas_call(head_kernel, grid=(1,), out_shape=(out_type, jax.ShapeDtyp...  10.6 us
    ppermute x6, waiting for transfers between devices, passed_along(): return lax.ppermute(array, ('blk', 'uly'), pairs)  9.71 us
    pallas_call x2, Pallas kernels, head_grads(): pl.pallas_call(tail_kernel, grid=(1,), out_shape=out_type, in_specs=[SMEM...  8.71 us
    pallas_call x2, Pallas kernels, packed(): pl.pallas_call(pack_kernel, grid=(steps,), out_shape=jax.ShapeDtypeStruct...  5.42 us
  transfers between devices with their start and end apart: 10, of which 10 were waited for; matrix products, arithmetic and copies ran while one was open for 1% of the time, Pallas kernels for 18%

profile of v5, /device:TPU:23, one launch (start us, length us, event | category | flops | bytes accessed | tf_op | source)
XLA Modules:
  0.0 202.9 jit_solution(10076088682548386752)
XLA Ops:
  0.6 2.7 %pack.3 = bf16[16,4,128,128]{3,2,1,0:T(8,128)(2,1)} custom-call(bf16[128,4096]{1,0:T(8,128)(2,1)} %refs_0_.3, bf16[128,4096]{1,0:T(8,128)(2,1)} %refs_1_.3, bf16[128,4096]{1,0:T(8,128)(2,1)} %refs_2_.3, bf16[128,4096]{1,0:T(8,128)(2,1)} %refs_3_.3), custom_call_target="tpu_custom_call" | custom-call | bytes 4194304 | tf_op jit(solution)/shard_map/pack/pallas_call | solution.py:219
  3.3 9.2 %all-to-all-start.2 = ((bf16[16,4,128,128]{3,2,1,0:T(8,128)(2,1)}), bf16[16,4,128,128]{3,2,1,0:T(8,128)(2,1)S(1)}, u32[]{:S(2)}, u32[]{:S(2)}) async-start(bf16[16,4,128,128]{3,2,1,0:T(8,128)(2,1)} %pack.3), calls=%async_computation.2 | async-start | bytes 4194304 | tf_op jit(solution)/shard_map/all_to_all | solution.py:342
  12.5 2.7 %pack.2 = bf16[16,4,128,128]{3,2,1,0:T(8,128)(2,1)} custom-call(bf16[128,4096]{1,0:T(8,128)(2,1)} %refs_0_.3, bf16[128,4096]{1,0:T(8,128)(2,1)} %refs_1_.3, bf16[128,4096]{1,0:T(8,128)(2,1)} %refs_2_.3, bf16[128,4096]{1,0:T(8,128)(2,1)} %refs_3_.3), custom_call_target="tpu_custom_call" | custom-call | bytes 4194304 | tf_op jit(solution)/shard_map/pack/pallas_call | solution.py:219
  15.2 46.2 %all-to-all-done.2.x_ref = bf16[16,4,128,128]{3,2,1,0:T(8,128)(2,1)S(1)} async-done(((bf16[16,4,128,128]{3,2,1,0:T(8,128)(2,1)}), bf16[16,4,128,128]{3,2,1,0:T(8,128)(2,1)S(1)}, u32[]{:S(2)}, u32[]{:S(2)}) %all-to-all-start.2) | async-done | bytes 2097184 | tf_op jit(solution)/shard_map/all_to_all | solution.py:342
  61.4 5.0 %all-to-all-start = ((bf16[16,4,128,128]{3,2,1,0:T(8,128)(2,1)}), bf16[16,4,128,128]{3,2,1,0:T(8,128)(2,1)}, u32[]{:S(2)}, u32[]{:S(2)}) async-start(bf16[16,4,128,128]{3,2,1,0:T(8,128)(2,1)} %pack.2), calls=%async_computation | async-start | bytes 4194304 | tf_op jit(solution)/shard_map/all_to_all | solution.py:342
  68.6 3.8 %collective-permute-start.4 = (bf16[7,2,128,128]{3,2,1,0:T(8,128)(2,1)S(1)}, bf16[7,2,128,128]{3,2,1,0:T(8,128)(2,1)S(1)}, u32[]{:S(2)}, u32[]{:S(2)}) collective-permute-start(bf16[7,2,128,128]{3,2,1,0:T(8,128)(2,1)S(1)} %slice.13), channel_id=1, source_target_pairs={{0,16},{1,17},{2,18},{3,19},{4,20},{5,21},{6,22},{7,23},{8,24},{9,... | collective-permute-start | bytes 1376264 | tf_op jit(solution)/shard_map/ppermute | solution.py:252
  72.3 7.8 %inner.3 = (bf16[16,3,128,128]{3,2,1,0:T(8,128)(2,1)}, f32[8,2,128,128]{3,2,1,0:T(8,128)}, f32[8,2,128,128]{3,2,1,0:T(8,128)}, bf16[7,2,128,128]{3,2,1,0:T(8,128)(2,1)}) custom-call(s32[18]{0:T(128)} %pad_add_fusion.st_ref, bf16[16,4,128,128]{3,2,1,0:T(8,128)(2,1)} %copy-done.2), custom_call_target="tpu_custom_call" | custom-call | flops 5000000000 | bytes 6291456 | tf_op jit(solution)/shard_map/inner/pallas_call | solution.py:262
  80.1 2.3 %collective-permute-start.3 = (bf16[7,2,128,128]{3,2,1,0:T(8,128)(2,1)}, bf16[7,2,128,128]{3,2,1,0:T(8,128)(2,1)S(1)}, u32[]{:S(2)}, u32[]{:S(2)}) collective-permute-start(bf16[7,2,128,128]{3,2,1,0:T(8,128)(2,1)} %get-tuple-element.27), channel_id=1, source_target_pairs={{16,0},{17,1},{18,2},{19,3},{20,4},{21,5},{22,6},{23,7},{24,8},{25... | collective-permute-start | bytes 1376264 | tf_op jit(solution)/shard_map/ppermute | solution.py:252
  84.9 6.0 %head.3 = (bf16[16,3,128,128]{3,2,1,0:T(8,128)(2,1)}, f32[4,8,256]{2,1,0:T(8,128)}) custom-call(s32[18]{0:T(128)} %pad_add_fusion.st_ref, bf16[16,4,128,128]{3,2,1,0:T(8,128)(2,1)} %copy-done.2, bf16[7,2,128,128]{3,2,1,0:T(8,128)(2,1)} %copy-done.5, f32[8,2,128,128]{3,2,1,0:T(8,128)} %get-tuple-element.28.head_ref, ...), custom_call_target="tpu_custom_call", output_to_operand_aliasing={{0}: (4, {})} | custom-call | flops 5000000000 | bytes 3145728 | tf_op jit(solution)/shard_map/head/pallas_call | solution.py:280
  90.8 4.8 %collective-permute-start.5 = (f32[4,8,256]{2,1,0:T(8,128)}, f32[4,8,256]{2,1,0:T(8,128)S(1)}, u32[]{:S(2)}, u32[]{:S(2)}) collective-permute-start(f32[4,8,256]{2,1,0:T(8,128)} %get-tuple-element.30), channel_id=1, source_target_pairs={{16,0},{17,1},{18,2},{19,3},{20,4},{21,5},{22,6},{23,7},{24,8},{25... | collective-permute-start | bytes 98312 | tf_op jit(solution)/shard_map/ppermute | solution.py:252
  96.3 1.8 collective-permute-done.5.stat_ref
  98.7 5.0 %tail.3 = bf16[16,3,128,128]{3,2,1,0:T(8,128)(2,1)} custom-call(s32[18]{0:T(128)} %pad_add_fusion.st_ref, bf16[16,4,128,128]{3,2,1,0:T(8,128)(2,1)} %copy-done.2, bf16[7,2,128,128]{3,2,1,0:T(8,128)(2,1)} %copy-done.4, f32[4,8,256]{2,1,0:T(8,128)} %copy-done.6, f32[8,2,128,128]{3,2,1,0:T(8,128)} %get-tuple-element.31.tail_ref, ...), custom_call_target="tpu_custom_call", output_to_operand_aliasing={{}: (5, {})} | custom-call | flops 2000000000 | bytes 3145728 | tf_op jit(solution)/shard_map/tail/pallas_call | solution.py:302
  103.7 11.8 %all-to-all-done.x_ref = bf16[16,4,128,128]{3,2,1,0:T(8,128)(2,1)} async-done(((bf16[16,4,128,128]{3,2,1,0:T(8,128)(2,1)}), bf16[16,4,128,128]{3,2,1,0:T(8,128)(2,1)}, u32[]{:S(2)}, u32[]{:S(2)}) %all-to-all-start) | async-done | bytes 2097184 | tf_op jit(solution)/shard_map/all_to_all | solution.py:342
  115.5 5.0 %all-to-all-start.3 = ((bf16[16,3,128,128]{3,2,1,0:T(8,128)(2,1)}), bf16[16,3,128,128]{3,2,1,0:T(8,128)(2,1)S(1)}, u32[]{:S(2)}, u32[]{:S(2)}) async-start(bf16[16,3,128,128]{3,2,1,0:T(8,128)(2,1)} %tail.3), calls=%async_computation.3 | async-start | bytes 3145728 | tf_op jit(solution)/shard_map/all_to_all | solution.py:342
  121.5 4.0 %collective-permute-start.1 = (bf16[7,2,128,128]{3,2,1,0:T(8,128)(2,1)S(1)}, bf16[7,2,128,128]{3,2,1,0:T(8,128)(2,1)S(1)}, u32[]{:S(2)}, u32[]{:S(2)}) collective-permute-start(bf16[7,2,128,128]{3,2,1,0:T(8,128)(2,1)S(1)} %slice.12), channel_id=1, source_target_pairs={{0,16},{1,17},{2,18},{3,19},{4,20},{5,21},{6,22},{7,23},{8,24},{9,... | collective-permute-start | bytes 1376264 | tf_op jit(solution)/shard_map/ppermute | solution.py:252
  125.5 5.9 %inner.2 = (bf16[16,3,128,128]{3,2,1,0:T(8,128)(2,1)S(1)}, f32[8,2,128,128]{3,2,1,0:T(8,128)S(1)}, f32[8,2,128,128]{3,2,1,0:T(8,128)S(1)}, bf16[7,2,128,128]{3,2,1,0:T(8,128)(2,1)S(1)}) custom-call(s32[18]{0:T(128)S(1)} %copy-done.1, bf16[16,4,128,128]{3,2,1,0:T(8,128)(2,1)} %all-to-all-done.x_ref), custom_call_target="tpu_custom_call" | custom-call | flops 5000000000 | bytes 6291456 | tf_op jit(solution)/shard_map/inner/pallas_call | solution.py:262
  131.5 2.4 %collective-permute-start = (bf16[7,2,128,128]{3,2,1,0:T(8,128)(2,1)S(1)}, bf16[7,2,128,128]{3,2,1,0:T(8,128)(2,1)S(1)}, u32[]{:S(2)}, u32[]{:S(2)}) collective-permute-start(bf16[7,2,128,128]{3,2,1,0:T(8,128)(2,1)S(1)} %get-tuple-element.21), channel_id=1, source_target_pairs={{16,0},{17,1},{18,2},{19,3},{20,4},{21,5},{22,6},{23,7},{24,8},{25... | collective-permute-start | bytes 1376264 | tf_op jit(solution)/shard_map/ppermute | solution.py:252
  133.9 3.1 %collective-permute-done.1.far_ref = bf16[7,2,128,128]{3,2,1,0:T(8,128)(2,1)S(1)} collective-permute-done((bf16[7,2,128,128]{3,2,1,0:T(8,128)(2,1)S(1)}, bf16[7,2,128,128]{3,2,1,0:T(8,128)(2,1)S(1)}, u32[]{:S(2)}, u32[]{:S(2)}) %collective-permute-start.1) | collective-permute-done | bytes 458784 | tf_op jit(solution)/shard_map/ppermute | solution.py:252
  137.0 4.6 %head.2 = (bf16[16,3,128,128]{3,2,1,0:T(8,128)(2,1)S(1)}, f32[4,8,256]{2,1,0:T(8,128)S(1)}) custom-call(s32[18]{0:T(128)S(1)} %copy-done.1, bf16[16,4,128,128]{3,2,1,0:T(8,128)(2,1)} %all-to-all-done.x_ref, bf16[7,2,128,128]{3,2,1,0:T(8,128)(2,1)S(1)} %collective-permute-done.1.far_ref, ...), custom_call_target="tpu_custom_call", output_to_operand_aliasing={{0}: (4, {})} | custom-call | flops 5000000000 | bytes 3145728 | tf_op jit(solution)/shard_map/head/pallas_call | solution.py:280
  141.6 4.8 %collective-permute-start.2 = (f32[4,8,256]{2,1,0:T(8,128)S(1)}, f32[4,8,256]{2,1,0:T(8,128)S(1)}, u32[]{:S(2)}, u32[]{:S(2)}) collective-permute-start(f32[4,8,256]{2,1,0:T(8,128)S(1)} %get-tuple-element.24), channel_id=1, source_target_pairs={{16,0},{17,1},{18,2},{19,3},{20,4},{21,5},{22,6},{23,7},{24,8},{25... | collective-permute-start | bytes 98312 | tf_op jit(solution)/shard_map/ppermute | solution.py:252
  149.0 3.7 %tail.2 = bf16[16,3,128,128]{3,2,1,0:T(8,128)(2,1)S(1)} custom-call(s32[18]{0:T(128)S(1)} %copy-done.1, bf16[16,4,128,128]{3,2,1,0:T(8,128)(2,1)} %all-to-all-done.x_ref, bf16[7,2,128,128]{3,2,1,0:T(8,128)(2,1)S(1)} %collective-permute-done.near_ref, f32[4,8,256]{2,1,0:T(8,128)S(1)} %collective-permute-done.2.stat_ref, ...), custom_call_target="tpu_custom_call", output_to_operand_aliasing={{}: (5, {})} | custom-call | flops 2000000000 | bytes 3145728 | tf_op jit(solution)/shard_map/tail/pallas_call | solution.py:302
  153.9 5.0 %all-to-all-done.3.back_ref = bf16[16,3,128,128]{3,2,1,0:T(8,128)(2,1)S(1)} async-done(((bf16[16,3,128,128]{3,2,1,0:T(8,128)(2,1)}), bf16[16,3,128,128]{3,2,1,0:T(8,128)(2,1)S(1)}, u32[]{:S(2)}, u32[]{:S(2)}) %all-to-all-start.3) | async-done | bytes 1572896 | tf_op jit(solution)/shard_map/all_to_all | solution.py:342
  158.9 4.3 %all-to-all-start.1 = ((bf16[16,3,128,128]{3,2,1,0:T(8,128)(2,1)}), bf16[16,3,128,128]{3,2,1,0:T(8,128)(2,1)S(1)}, u32[]{:S(2)}, u32[]{:S(2)}) async-start(bf16[16,3,128,128]{3,2,1,0:T(8,128)(2,1)} %copy-done), calls=%async_computation.1 | async-start | bytes 3145728 | tf_op jit(solution)/shard_map/all_to_all | solution.py:342
  164.5 37.1 %all-to-all-done.1.back_ref = bf16[16,3,128,128]{3,2,1,0:T(8,128)(2,1)S(1)} async-done(((bf16[16,3,128,128]{3,2,1,0:T(8,128)(2,1)}), bf16[16,3,128,128]{3,2,1,0:T(8,128)(2,1)S(1)}, u32[]{:S(2)}, u32[]{:S(2)}) %all-to-all-start.1) | async-done | bytes 1572896 | tf_op jit(solution)/shard_map/all_to_all | solution.py:342
  (25 shorter events, 12.6 us)
Async XLA Ops:
  3.3 58.1 %all-to-all-start.2 = ((bf16[16,4,128,128]{3,2,1,0:T(8,128)(2,1)}), bf16[16,4,128,128]{3,2,1,0:T(8,128)(2,1)S(1)}, u32[]{:S(2)}, u32[]{:S(2)}) async-start(bf16[16,4,128,128]{3,2,1,0:T(8,128)(2,1)} %pack.3), calls=%async_computation.2 | async-start | bytes 4194304 | tf_op jit(solution)/shard_map/all_to_all | solution.py:342
  15.2 51.2 %copy-start.3 = (s32[256]{0:T(256)S(1)}, s32[256]{0:T(256)}, u32[]{:S(2)}) copy-start(s32[256]{0:T(256)} %param.9) | copy-start | bytes 3076
  61.4 7.1 %copy-start.2 = (bf16[16,4,128,128]{3,2,1,0:T(8,128)(2,1)}, bf16[16,4,128,128]{3,2,1,0:T(8,128)(2,1)S(1)}, u32[]{:S(2)}) copy-start(bf16[16,4,128,128]{3,2,1,0:T(8,128)(2,1)S(1)} %all-to-all-done.2.x_ref) | copy-start | bytes 6291460
  61.4 54.0 %all-to-all-start = ((bf16[16,4,128,128]{3,2,1,0:T(8,128)(2,1)}), bf16[16,4,128,128]{3,2,1,0:T(8,128)(2,1)}, u32[]{:S(2)}, u32[]{:S(2)}) async-start(bf16[16,4,128,128]{3,2,1,0:T(8,128)(2,1)} %pack.2), calls=%async_computation | async-start | bytes 4194304 | tf_op jit(solution)/shard_map/all_to_all | solution.py:342
  68.6 15.5 %collective-permute-start.4 = (bf16[7,2,128,128]{3,2,1,0:T(8,128)(2,1)S(1)}, bf16[7,2,128,128]{3,2,1,0:T(8,128)(2,1)S(1)}, u32[]{:S(2)}, u32[]{:S(2)}) collective-permute-start(bf16[7,2,128,128]{3,2,1,0:T(8,128)(2,1)S(1)} %slice.13), channel_id=1, source_target_pairs={{0,16},{1,17},{2,18},{3,19},{4,20},{5,21},{6,22},{7,23},{8,24},{9,... | collective-permute-start | bytes 1376264 | tf_op jit(solution)/shard_map/ppermute | solution.py:252
  80.1 16.1 %collective-permute-start.3 = (bf16[7,2,128,128]{3,2,1,0:T(8,128)(2,1)}, bf16[7,2,128,128]{3,2,1,0:T(8,128)(2,1)S(1)}, u32[]{:S(2)}, u32[]{:S(2)}) collective-permute-start(bf16[7,2,128,128]{3,2,1,0:T(8,128)(2,1)} %get-tuple-element.27), channel_id=1, source_target_pairs={{16,0},{17,1},{18,2},{19,3},{20,4},{21,5},{22,6},{23,7},{24,8},{25... | collective-permute-start | bytes 1376264 | tf_op jit(solution)/shard_map/ppermute | solution.py:252
  84.0 0.8 copy-start.5
  90.8 7.3 %collective-permute-start.5 = (f32[4,8,256]{2,1,0:T(8,128)}, f32[4,8,256]{2,1,0:T(8,128)S(1)}, u32[]{:S(2)}, u32[]{:S(2)}) collective-permute-start(f32[4,8,256]{2,1,0:T(8,128)} %get-tuple-element.30), channel_id=1, source_target_pairs={{16,0},{17,1},{18,2},{19,3},{20,4},{21,5},{22,6},{23,7},{24,8},{25... | collective-permute-start | bytes 98312 | tf_op jit(solution)/shard_map/ppermute | solution.py:252
  96.3 1.8 copy-start.4
  98.1 0.6 copy-start.6
  103.7 21.8 %copy-start.1 = (s32[18]{0:T(128)S(1)}, s32[18]{0:T(128)}, u32[]{:S(2)}) copy-start(s32[18]{0:T(128)} %pad_add_fusion.st_ref) | copy-start | bytes 220
  115.5 43.4 %all-to-all-start.3 = ((bf16[16,3,128,128]{3,2,1,0:T(8,128)(2,1)}), bf16[16,3,128,128]{3,2,1,0:T(8,128)(2,1)S(1)}, u32[]{:S(2)}, u32[]{:S(2)}) async-start(bf16[16,3,128,128]{3,2,1,0:T(8,128)(2,1)} %tail.3), calls=%async_computation.3 | async-start | bytes 3145728 | tf_op jit(solution)/shard_map/all_to_all | solution.py:342
  121.5 15.5 %collective-permute-start.1 = (bf16[7,2,128,128]{3,2,1,0:T(8,128)(2,1)S(1)}, bf16[7,2,128,128]{3,2,1,0:T(8,128)(2,1)S(1)}, u32[]{:S(2)}, u32[]{:S(2)}) collective-permute-start(bf16[7,2,128,128]{3,2,1,0:T(8,128)(2,1)S(1)} %slice.12), channel_id=1, source_target_pairs={{0,16},{1,17},{2,18},{3,19},{4,20},{5,21},{6,22},{7,23},{8,24},{9,... | collective-permute-start | bytes 1376264 | tf_op jit(solution)/shard_map/ppermute | solution.py:252
  131.5 16.1 %collective-permute-start = (bf16[7,2,128,128]{3,2,1,0:T(8,128)(2,1)S(1)}, bf16[7,2,128,128]{3,2,1,0:T(8,128)(2,1)S(1)}, u32[]{:S(2)}, u32[]{:S(2)}) collective-permute-start(bf16[7,2,128,128]{3,2,1,0:T(8,128)(2,1)S(1)} %get-tuple-element.21), channel_id=1, source_target_pairs={{16,0},{17,1},{18,2},{19,3},{20,4},{21,5},{22,6},{23,7},{24,8},{25... | collective-permute-start | bytes 1376264 | tf_op jit(solution)/shard_map/ppermute | solution.py:252
  141.6 7.4 %collective-permute-start.2 = (f32[4,8,256]{2,1,0:T(8,128)S(1)}, f32[4,8,256]{2,1,0:T(8,128)S(1)}, u32[]{:S(2)}, u32[]{:S(2)}) collective-permute-start(f32[4,8,256]{2,1,0:T(8,128)S(1)} %get-tuple-element.24), channel_id=1, source_target_pairs={{16,0},{17,1},{18,2},{19,3},{20,4},{21,5},{22,6},{23,7},{24,8},{25... | collective-permute-start | bytes 98312 | tf_op jit(solution)/shard_map/ppermute | solution.py:252
  152.7 1.2 copy-start
  158.9 42.7 %all-to-all-start.1 = ((bf16[16,3,128,128]{3,2,1,0:T(8,128)(2,1)}), bf16[16,3,128,128]{3,2,1,0:T(8,128)(2,1)S(1)}, u32[]{:S(2)}, u32[]{:S(2)}) async-start(bf16[16,3,128,128]{3,2,1,0:T(8,128)(2,1)} %copy-done), calls=%async_computation.1 | async-start | bytes 3145728 | tf_op jit(solution)/shard_map/all_to_all | solution.py:342
